TPU v7x, 32 devices: a whole 2x2x4 slice. The times are simulated.
32 devices in a mesh: groups: 2 (over y), tile: 4 (over z), dither: 2 (over x), band: 2 (over core).
Axes of the slice: x: 2, y: 2, z: 4, core: 2. Of those that a mesh axis runs over, the one named last changes fastest.
Arguments:
- spectra: bfloat16 [2048, 1024], P(('groups', 'tile'), 'band'), parts along dimension 0, may hold values from -6 to 6
- psf_blocks: bfloat16 [16, 128, 128], replicated, may hold values from -0.5 to 0.5
- observed: bfloat16 [4, 4096, 128], P(('groups', 'dither'), 'tile'), parts along dimension 0, may hold values from -6 to 6
- bad_mask: int32 [4, 4096, 128], P(('groups', 'dither'), 'tile'), parts along dimension 0, may hold values 0 or 1
- trace_tile: int32 [32768, 1], P(('groups', 'tile', 'dither', 'band')), parts along dimension 0, may hold values from 0 to 3; in each aligned block of 1024 rows (0 to 1023, 1024 to 2047, ...) at most 512 rows name the same one
- trace_slot: int32 [32768], P(('groups', 'tile', 'dither', 'band')), parts along dimension 0, may hold values from 0 to 1023
- trace_source: int32 [32768, 1], P(('groups', 'tile', 'dither', 'band')), parts along dimension 0, may hold values from 0 to 255; in each aligned block of 1024 rows (0 to 1023, 1024 to 2047, ...) at most 8 rows name the same one
- trace_block: int32 [32768], P(('groups', 'tile', 'dither', 'band')), parts along dimension 0, may hold values from 0 to 3
- psf_index: int32 [32768], P(('groups', 'tile', 'dither', 'band')), parts along dimension 0, may hold values from 0 to 15
Outputs:
- gradient: float32 [2048, 1024], P(('groups', 'tile', 'dither'), 'band'), parts along dimension 0
- residual: bfloat16 [4, 4096, 128], P(('groups', 'dither'), 'tile'), parts along dimension 0
There are 2 independent parts, one for each index of `groups`. A program takes and returns all parts, laid end to end along the dimension named above; an argument that names none is the same for every part. Nothing has to cross between parts.
Inputs may be any that keep to these rules, and one draw needn't show every extreme that they name: `trace_tile`: among the trace blocks of one sky region, dither and wavelength half, at most 512 name the same tile, and in every draw some tile is named by exactly 512 of them for some such group. `trace_source`: among the trace blocks of one sky region, dither and wavelength half, at most 8 name the same source, and in every draw some source is named by exactly 8 of them for some such group.
All inputs are finite; a program needn't handle non-finite values. No bound on the sum of `bad_mask` on one device may be relied on, other than what follows from the above.
Results may differ from a plain program's by a relative error of at most 0.006.
Values may be sent and summed in bfloat16 or wider, within the bound.
A program may use at most 64 MiB of HBM per device.

v0:
```python
import math

import jax
import jax.numpy as jnp
from jax import lax
from jax.sharding import PartitionSpec as P


def in_blocks(worker, values, kinds):
    row_count = values.shape[0]
    block_size = math.gcd(row_count, 512)
    result = lax.map(
        worker,
        (
            values.reshape(row_count // block_size, block_size, values.shape[1]),
            kinds.reshape(row_count // block_size, block_size),
        ),
    )
    return result.reshape(row_count, result.shape[-1])


def through_table(values, kinds, psf_blocks):
    table_count, bin_count, pixel_count = psf_blocks.shape
    flat_table = psf_blocks.reshape(table_count * bin_count, pixel_count)

    def through_single(inputs):
        part_values, part_kinds = inputs
        chosen = (
            part_kinds[:, None, None] == jnp.arange(table_count, dtype=jnp.int32)[None, :, None]
        )
        spread = jnp.where(chosen, part_values[:, None, :], jnp.zeros((), jnp.bfloat16))
        spread = spread.reshape(part_values.shape[0], table_count * bin_count)
        return jnp.dot(spread, flat_table, preferred_element_type=jnp.float32)

    return in_blocks(through_single, values, kinds)


def back_through_table(values, kinds, psf_blocks):
    table_count, bin_count, pixel_count = psf_blocks.shape
    back_table = psf_blocks.transpose(2, 0, 1).reshape(pixel_count, table_count * bin_count)

    def back_single(inputs):
        part_values, part_kinds = inputs
        product = jnp.dot(part_values, back_table, preferred_element_type=jnp.float32)
        product = product.reshape(part_values.shape[0], table_count, bin_count)
        chosen = (
            part_kinds[:, None, None] == jnp.arange(table_count, dtype=jnp.int32)[None, :, None]
        )
        return jnp.sum(jnp.where(chosen, product, 0.0), axis=1)

    return in_blocks(back_single, values, kinds)


def slot_positions(target, group_count):
    member = (target[:, None] == jnp.arange(group_count, dtype=jnp.int32)[None, :]).astype(
        jnp.int32
    )
    return jnp.sum((jnp.cumsum(member, axis=0) - 1) * member, axis=1)


def per_device(
    spectra,
    psf_blocks,
    observed,
    bad_mask,
    trace_tile,
    trace_slot,
    trace_source,
    trace_block,
    psf_index,
):
    tile_count = lax.axis_size("tile")
    entry_count = trace_slot.shape[0]
    capacity = 2 * entry_count // tile_count
    table_count, bin_count, pixel_count = psf_blocks.shape
    source_count = spectra.shape[0]
    block_count = spectra.shape[1] // bin_count
    slot_count = observed.shape[1]
    target = trace_tile[:, 0]
    source_local = trace_source[:, 0]
    position = slot_positions(target, tile_count)
    spec_rows = source_local * block_count + trace_block
    spec_values = spectra.reshape(source_count * block_count, bin_count)[spec_rows]
    send_slots = jnp.zeros((tile_count, capacity), jnp.int32).at[target, position].set(trace_slot)
    send_values = (
        jnp.zeros((tile_count, capacity, bin_count), jnp.bfloat16)
        .at[target, position]
        .set(spec_values)
    )
    send_kinds = jnp.zeros((tile_count, capacity), jnp.int32).at[target, position].set(psf_index)
    got_values, got_slots, got_kinds = (
        lax.all_to_all(send_values, "tile", split_axis=0, concat_axis=0, tiled=True),
        lax.all_to_all(send_slots, "tile", split_axis=0, concat_axis=0, tiled=True),
        lax.all_to_all(send_kinds, "tile", split_axis=0, concat_axis=0, tiled=True),
    )
    flat_kinds = got_kinds.reshape(tile_count * capacity)
    flat_traces = through_table(
        got_values.reshape(tile_count * capacity, bin_count), flat_kinds, psf_blocks
    ).astype(jnp.bfloat16)
    flat_slots = got_slots.reshape(tile_count * capacity)
    partial_value = jax.ops.segment_sum(flat_traces.astype(jnp.float32), flat_slots, slot_count)
    model_image = lax.psum(partial_value, "band")
    residual = (
        bad_mask[0].astype(jnp.float32) * (model_image - observed[0].astype(jnp.float32))
    ).astype(jnp.bfloat16)
    under_rows = residual[flat_slots]
    owner_terms = back_through_table(under_rows, flat_kinds, psf_blocks)
    returned = lax.all_to_all(
        owner_terms.reshape(tile_count, capacity, bin_count).astype(jnp.bfloat16),
        "tile",
        split_axis=0,
        concat_axis=0,
        tiled=True,
    ).astype(jnp.float32)
    grad_terms = returned[target, position]
    local_grad = jax.ops.segment_sum(grad_terms, spec_rows, source_count * block_count)
    local_grad = local_grad.reshape(source_count, block_count * bin_count)
    gradient = lax.psum_scatter(local_grad, "dither", scatter_dimension=0, tiled=True)
    return (gradient, residual[None])


def solution(mesh):
    in_specs = (
        P(("groups", "tile"), "band"),
        P(),
        P(("groups", "dither"), "tile", None),
        P(("groups", "dither"), "tile", None),
        P(("groups", "tile", "dither", "band"), None),
        P(("groups", "tile", "dither", "band")),
        P(("groups", "tile", "dither", "band"), None),
        P(("groups", "tile", "dither", "band")),
        P(("groups", "tile", "dither", "band")),
    )
    out_specs = (P(("groups", "tile", "dither"), "band"), P(("groups", "dither"), "tile", None))
    return jax.shard_map(
        per_device, mesh=mesh, in_specs=in_specs, out_specs=out_specs, check_vma=False
    )
```

profile of v0, /device:TPU:0, one launch (start us, length us, event | category | flops | bytes accessed | tf_op | source)
XLA Modules:
  0.0 172.2 jit_solution(7300409605480088494)
XLA Ops:
  7.2 0.7 fusion.25
  7.9 1.1 reduce-window.6
  9.1 0.2 slice_reduce_fusion
  9.3 0.2 reduce-window.9
  9.4 0.1 add_bitcast_fusion
  9.5 0.7 fusion.24
  10.2 0.7 shift-left_or_fusion
  11.0 0.7 multiply_reduce_fusion
  11.7 0.8 and_reduce_fusion
  12.4 0.7 broadcast_multiply_fusion
  13.1 0.7 fusion.26
  13.8 5.0 %scatter_custom_fusion.2 = s32[2048]{0:T(1024)} fusion(s32[1024]{0:T(1024)S(1)} %get-tuple-element.83, s32[1024]{0:T(1024)} %param.21, s32[]{:T(128)} %copy.45), kind=kCustom, calls=%fused_computation.57 | custom fusion | bytes 8704
  18.9 6.3 %all-to-all-start = ((s32[4,1,512]{2,1,0:T(1,128)}), s32[4,1,512]{2,1,0:T(1,128)S(1)}, u32[]{:S(2)}, u32[]{:S(2)}) async-start(s32[4,1,512]{2,1,0:T(1,128)} %bitcast.14), calls=%async_computation | async-start | bytes 16384 | tf_op jit(solution)/shard_map/all_to_all | solution.py:94
  25.2 1.1 reshape.162
  26.3 7.0 %scatter_custom_fusion.4 = bf16[2048,128]{1,0:T(8,128)(2,1)} fusion(s32[1024]{0:T(1024)S(1)} %get-tuple-element.83, bf16[1024,128]{1,0:T(8,128)(2,1)S(1)} %reshape.162, s32[1024]{0:T(1024)S(1)} %get-tuple-element.78, bf16[]{:T(256)} %constant.45.clone.1), kind=kCustom, calls=%fused_computation.31 | custom fusion | bytes 524290
  33.4 5.1 %all-to-all-start.2 = ((bf16[4,512,128]{2,1,0:T(8,128)(2,1)}), bf16[4,512,128]{2,1,0:T(8,128)(2,1)S(1)}, u32[]{:S(2)}, u32[]{:S(2)}) async-start(bf16[4,512,128]{2,1,0:T(8,128)(2,1)} %bitcast.18), calls=%async_computation.2 | async-start | bytes 1048576 | tf_op jit(solution)/shard_map/all_to_all | solution.py:92
  38.5 5.0 %scatter_custom_fusion.3 = s32[2048]{0:T(1024)} fusion(s32[1024]{0:T(1024)S(1)} %get-tuple-element.83, s32[1024]{0:T(1024)} %param.18, s32[]{:T(128)} %copy.45), kind=kCustom, calls=%fused_computation.55 | custom fusion | bytes 8704
  43.5 8.9 %all-to-all-done.2 = bf16[4,512,128]{2,1,0:T(8,128)(2,1)S(1)} async-done(((bf16[4,512,128]{2,1,0:T(8,128)(2,1)}), bf16[4,512,128]{2,1,0:T(8,128)(2,1)S(1)}, u32[]{:S(2)}, u32[]{:S(2)}) %all-to-all-start.2) | async-done | bytes 524320 | tf_op jit(solution)/shard_map/all_to_all | solution.py:92
  52.4 3.2 %all-to-all-start.1 = ((s32[4,1,512]{2,1,0:T(1,128)}), s32[4,1,512]{2,1,0:T(1,128)S(1)}, u32[]{:S(2)}, u32[]{:S(2)}) async-start(s32[4,1,512]{2,1,0:T(1,128)} %bitcast.16), calls=%async_computation.1 | async-start | bytes 16384 | tf_op jit(solution)/shard_map/all_to_all | solution.py:93
  55.7 0.1 broadcast.114.clone
  55.8 14.7 %while.20 = (s32[]{:T(128)}, bf16[4,512,128]{2,1,0:T(8,128)(2,1)S(1)}, s32[4,512]{1,0:T(4,128)S(1)}, bf16[4,512,128]{2,1,0:T(8,128)(2,1)S(1)}, bf16[2048,128]{1,0:T(8,128)(2,1)S(1)}, /*index=5*/s32[]{:T(128)}) while((s32[]{:T(128)}, bf16[4,512,128]{2,1,0:T(8,128)(2,1)S(1)}, s32[4,512]{1,0:T(4,128)S(1)}, bf16[4,512,128]{2,1,0:T(8,128)(2,1)S(1)}, ...), condition=%wide.region_7.8_spmd, body=%wide.region_6.7_spmd.sunk | while | flops 269492224 | bytes 5396561 | solution.py:12
  55.9 0.1 iota_compare_fusion.6
  56.0 2.7 %broadcast_select_fusion.3 = bf16[512,16,128]{2,1,0:T(8,128)(2,1)S(1)} fusion(pred[512,16]{1,0:T(8,128)(4,1)S(1)} %iota_compare_fusion.6, bf16[512,128]{1,0:T(8,128)(2,1)S(1)} %dynamic-slice_bitcast_fusion.2), kind=kLoop, calls=%fused_computation.11.clone.1 | loop fusion | flops 1048576 | bytes 2236416 | tf_op jit(solution)/shard_map/while/body/eval_jaxpr/jit(_where)/select_n | solution.py:31
  58.7 0.8 fusion.40
  59.5 0.1 iota_compare_fusion.6
  59.7 2.7 %broadcast_select_fusion.3 = bf16[512,16,128]{2,1,0:T(8,128)(2,1)S(1)} fusion(pred[512,16]{1,0:T(8,128)(4,1)S(1)} %iota_compare_fusion.6, bf16[512,128]{1,0:T(8,128)(2,1)S(1)} %dynamic-slice_bitcast_fusion.2), kind=kLoop, calls=%fused_computation.11.clone.1 | loop fusion | flops 1048576 | bytes 2236416 | tf_op jit(solution)/shard_map/while/body/eval_jaxpr/jit(_where)/select_n | solution.py:31
  62.4 0.8 fusion.40
  63.2 0.1 iota_compare_fusion.6
  63.3 2.7 %broadcast_select_fusion.3 = bf16[512,16,128]{2,1,0:T(8,128)(2,1)S(1)} fusion(pred[512,16]{1,0:T(8,128)(4,1)S(1)} %iota_compare_fusion.6, bf16[512,128]{1,0:T(8,128)(2,1)S(1)} %dynamic-slice_bitcast_fusion.2), kind=kLoop, calls=%fused_computation.11.clone.1 | loop fusion | flops 1048576 | bytes 2236416 | tf_op jit(solution)/shard_map/while/body/eval_jaxpr/jit(_where)/select_n | solution.py:31
  66.0 0.8 fusion.40
  66.9 0.1 iota_compare_fusion.6
  67.0 2.7 %broadcast_select_fusion.3 = bf16[512,16,128]{2,1,0:T(8,128)(2,1)S(1)} fusion(pred[512,16]{1,0:T(8,128)(4,1)S(1)} %iota_compare_fusion.6, bf16[512,128]{1,0:T(8,128)(2,1)S(1)} %dynamic-slice_bitcast_fusion.2), kind=kLoop, calls=%fused_computation.11.clone.1 | loop fusion | flops 1048576 | bytes 2236416 | tf_op jit(solution)/shard_map/while/body/eval_jaxpr/jit(_where)/select_n | solution.py:31
  69.7 0.8 fusion.40
  70.5 13.9 %scatter_custom_fusion = f32[1024,128]{1,0:T(8,128)} fusion(s32[2048]{0:T(1024)S(1)} %bitcast.100, bf16[2048,128]{1,0:T(8,128)(2,1)S(1)} %bitcast.93, f32[]{:T(128)} %constant.24.clone.1), kind=kCustom, calls=%fused_computation.24 | custom fusion | flops 524288 | bytes 1048580 | tf_op jit(solution)/shard_map/scatter-add | solution.py:101
  84.6 21.0 %all-reduce.2.cloned.1.call-done = f32[1024,128]{1,0:T(8,128)} async-done(((f32[1024,128]{1,0:T(8,128)}), f32[1024,128]{1,0:T(8,128)}) %all-reduce.2.cloned.1.call-update) | async-done | bytes 524304 | tf_op jit(solution)/shard_map/psum | solution.py:102
  105.5 1.1 fusion.15
  106.7 6.2 %gather_fusion = bf16[2048,128]{1,0:T(8,128)(2,1)S(1)} fusion(bf16[1024,128]{1,0:T(8,128)(2,1)S(1)} %fusion.15, s32[2048]{0:T(1024)S(1)} %broadcast_clamp_fusion), kind=kCustom, calls=%fused_computation.1 | custom fusion | bytes 1056768 | tf_op jit(solution)/shard_map/gather | solution.py:106
  112.9 0.1 broadcast.114
  113.0 6.5 %while.21 = (s32[]{:T(128)}, bf16[4,512,128]{2,1,0:T(8,128)(2,1)S(1)}, s32[4,512]{1,0:T(4,128)S(1)}, bf16[4,512,128]{2,1,0:T(8,128)(2,1)S(1)}, bf16[128,2048]{0,1:T(8,128)(2,1)S(1)}, /*index=5*/s32[]{:T(128)}) while((s32[]{:T(128)}, bf16[4,512,128]{2,1,0:T(8,128)(2,1)S(1)}, s32[4,512]{1,0:T(4,128)S(1)}, ...), condition=%wide.region_12.13_spmd, body=%wide.region_10.12_spmd.sunk | while | flops 270475264 | bytes 1071185 | solution.py:12
  113.0 1.6 select_reduce_fusion.2
  114.6 1.5 select_reduce_fusion.2
  116.3 1.5 select_reduce_fusion.2
  117.9 1.5 select_reduce_fusion.2
  119.5 19.6 %all_to_all.31 = bf16[4,512,128]{2,1,0:T(8,128)(2,1)S(1)} all-to-all(bf16[4,512,128]{2,1,0:T(8,128)(2,1)S(1)} %get-tuple-element.57), channel_id=1, replica_groups=mesh['groups'=2,'tile'=4,'dither'=2,'band'=2] {'tile'}, dimensions={0} | all-to-all | bytes 1048576 | tf_op jit(solution)/shard_map/all_to_all | solution.py:108
  139.1 0.1 convert_element_type.46
  139.2 11.6 %scatter_custom_fusion.1 = f32[1024,128]{1,0:T(8,128)S(1)} fusion(s32[1024]{0:T(1024)S(1)} %get-tuple-element.79, f32[4,512,128]{2,1,0:T(8,128)S(1)} %convert_element_type.46, s32[1024]{0:T(1024)S(1)} %bitcast.106, f32[]{:T(128)} %constant.24.clone.1), kind=kCustom, calls=%fused_computation.29 | custom fusion | flops 131072 | bytes 524292 | tf_op jit(solution)/shard_map/scatter-add | solution.py:116
  150.8 0.9 reshape.166
  151.7 13.7 %reduce-scatter.2.cloned.1.call-done = f32[128,512]{1,0:T(8,128)} async-done(((f32[256,512]{1,0:T(8,128)}), f32[128,512]{1,0:T(8,128)}) %reduce-scatter.2.cloned.1.call-update) | async-done | bytes 262160 | tf_op jit(solution)/shard_map/reduce_scatter | solution.py:118
  (37 shorter events, 0.4 us)
Async XLA Ops:
  7.2 48.6 %copy-start.3 = (bf16[16,128,128]{2,1,0:T(8,128)(2,1)S(1)}, bf16[16,128,128]{2,1,0:T(8,128)(2,1)}, u32[]{:S(2)}) copy-start(bf16[16,128,128]{2,1,0:T(8,128)(2,1)} %param.14) | copy-start | bytes 1572868
  18.9 14.5 %all-to-all-start = ((s32[4,1,512]{2,1,0:T(1,128)}), s32[4,1,512]{2,1,0:T(1,128)S(1)}, u32[]{:S(2)}, u32[]{:S(2)}) async-start(s32[4,1,512]{2,1,0:T(1,128)} %bitcast.14), calls=%async_computation | async-start | bytes 16384 | tf_op jit(solution)/shard_map/all_to_all | solution.py:94
  33.4 19.0 %all-to-all-start.2 = ((bf16[4,512,128]{2,1,0:T(8,128)(2,1)}), bf16[4,512,128]{2,1,0:T(8,128)(2,1)S(1)}, u32[]{:S(2)}, u32[]{:S(2)}) async-start(bf16[4,512,128]{2,1,0:T(8,128)(2,1)} %bitcast.18), calls=%async_computation.2 | async-start | bytes 1048576 | tf_op jit(solution)/shard_map/all_to_all | solution.py:92
  52.4 18.1 %all-to-all-start.1 = ((s32[4,1,512]{2,1,0:T(1,128)}), s32[4,1,512]{2,1,0:T(1,128)S(1)}, u32[]{:S(2)}, u32[]{:S(2)}) async-start(s32[4,1,512]{2,1,0:T(1,128)} %bitcast.16), calls=%async_computation.1 | async-start | bytes 16384 | tf_op jit(solution)/shard_map/all_to_all | solution.py:93
  55.6 49.9 %all-reduce.2.cloned.1.call-start = ((), (), s32[]{:S(2)}) async-start(), calls=%async_computation.5 | async-start | bytes 1048576 | tf_op jit(solution)/shard_map/psum | solution.py:102
  55.8 49.7 %copy-start.1 = (s32[1,1024,128]{2,1,0:T(8,128)S(1)}, s32[1,1024,128]{2,1,0:T(8,128)}, u32[]{:S(2)}) copy-start(s32[1,1024,128]{2,1,0:T(8,128)} %param.16) | copy-start | bytes 1572868
  55.8 49.7 %copy-start.2 = (bf16[1,1024,128]{2,1,0:T(8,128)(2,1)S(1)}, bf16[1,1024,128]{2,1,0:T(8,128)(2,1)}, u32[]{:S(2)}) copy-start(bf16[1,1024,128]{2,1,0:T(8,128)(2,1)} %param.15) | copy-start | bytes 786436
  84.5 80.9 %reduce-scatter.2.cloned.1.call-start = ((), (), s32[]{:S(2)}) async-start(), calls=%async_computation.6 | async-start | bytes 786432 | tf_op jit(solution)/shard_map/reduce_scatter | solution.py:118
  106.7 6.2 %copy-start = (bf16[1024,128]{1,0:T(8,128)(2,1)}, bf16[1024,128]{1,0:T(8,128)(2,1)S(1)}, u32[]{:S(2)}) copy-start(bf16[1024,128]{1,0:T(8,128)(2,1)S(1)} %fusion.15) | copy-start | bytes 786436
Sparse Core Ops, SparseCore 0:
  84.6 20.8 all-reduce.1
  151.8 13.5 reduce-scatter.1
where the time goes:
time: 172 us
  other arithmetic  44.5 us (26%)
  waiting for transfers between devices  43.6 us (25%)
  local copies, waits for them, and re-layouts  25.9 us (15%)
  blocking collectives  19.6 us (11%)
  starting transfers between devices  14.7 us (9%)
  between operations  14.2 us (8%)
  matrix products  9.29 us (5%)
    psum x1, waiting for transfers between devices, per_device(): model_image = lax.psum(partial_value, 'band')  21 us
    all_to_all x1, blocking collectives, per_device(): lax.all_to_all(owner_terms.reshape(tile_count, capacity, bin_count).astyp...  19.6 us
    unnamed x12, local copies, waits for them, and re-layouts  17.2 us
    scatter-add x1, other arithmetic, per_device(): jax.ops.segment_sum(flat_traces.astype(jnp.float32), flat_slots, slot_count)  13.9 us
    reduce_scatter x1, waiting for transfers between devices, per_device(): lax.psum_scatter(local_grad, 'dither', scatter_dimension=0, tiled=True)  13.7 us
    scatter-add x1, other arithmetic, per_device(): jax.ops.segment_sum(grad_terms, spec_rows, source_count * block_count)  11.6 us
    select_n x4, other arithmetic, through_single(): jnp.where(chosen, part_values[:, None, :], jnp.zeros((), jnp.bfloat16))  10.8 us
    all_to_all x1, waiting for transfers between devices, per_device(): lax.all_to_all(send_values, 'tile', split_axis=0, concat_axis=0, tiled=True)  8.89 us
  transfers between devices with their start and end apart: 5, of which 3 were waited for; matrix products, arithmetic and copies ran while one was open for 16% of the time, Pallas kernels for 0%

commit v1 on v0

v1 whole, which is shorter than its diff:
```python
import functools

import jax
import jax.numpy as jnp
from jax import lax
from jax.experimental import pallas as pl
from jax.experimental.pallas import tpu as pltpu
from jax.sharding import PartitionSpec as P

MESH = pl.DeviceIdType.MESH
F32, BF16 = jnp.float32, jnp.bfloat16


def dot(a, b):
    return jnp.dot(a, b, preferred_element_type=F32)


def kernel(
    cfg,
    spectra_ref, psf_ref, obs_ref, bad_ref, tile_ref, slot_ref, src_ref, blk_ref, kind_ref,
    grad_ref, res_ref,
    cols, traces, masked, onehot, onehot_t, psf_t, own, fsend, frecv, zrecv, zsend,
    resid, rows, terms, dsend, drecv,
    fs_sem, fr_sem, zs_sem, zr_sem, gs_sem, gr_sem, ps_sem, pr_sem, ds_sem, dr_sem,
):
    n, nd, parts, sub = cfg
    entries = tile_ref.shape[1]
    slots = obs_ref.shape[0]
    half = slots // 2
    kinds, bins, pixels = psf_ref.shape
    sources, wide = spectra_ref.shape
    blocks = wide // bins
    step_rows = min(256, entries)
    z = lax.axis_index("tile")
    b = lax.axis_index("band")
    d = lax.axis_index("dither")
    peer = {"band": 1 - b}
    above, below = {"tile": z + 1}, {"tile": z - 1}
    has_above, has_below = z < n - 1, z > 0

    barrier = pltpu.get_barrier_semaphore()

    def greet(where):
        pl.semaphore_signal(barrier, inc=1, device_id=where, device_id_type=MESH)

    greet(peer)
    pl.when(has_above)(lambda: greet(above))
    pl.when(has_below)(lambda: greet(below))
    for k in range(1, nd):
        greet({"dither": lax.rem(d + k, nd)})

    stack = [tile_ref[...], slot_ref[...], src_ref[...], blk_ref[...], kind_ref[...]]
    cols[...] = jnp.concatenate(stack + [kind_ref[...]] * 3, axis=0).T

    def spread(values, which, count):
        return jnp.concatenate(
            [jnp.where(which == k, values, 0.0).astype(BF16) for k in range(count)], axis=1
        )

    def forward(i, _):
        at = pl.ds(pl.multiple_of(i * step_rows, step_rows), step_rows)
        col = cols[at, :]
        lane = lax.broadcasted_iota(jnp.int32, (step_rows, sources), 1)
        pick = jnp.where(lane == col[:, 2:3], 1.0, 0.0).astype(BF16)
        found = dot(pick, spectra_ref[...])
        block = jnp.broadcast_to(col[:, 3:4], (step_rows, bins))
        value = jnp.zeros((step_rows, bins), F32)
        for k in range(blocks):
            value = jnp.where(block == k, found[:, k * bins:(k + 1) * bins], value)
        kind = jnp.broadcast_to(col[:, 4:5], (step_rows, bins))
        table = psf_ref[...].reshape(kinds * bins, pixels)
        traces[at, :] = dot(spread(value, kind, kinds), table).astype(BF16)
        return _

    lax.fori_loop(0, entries // step_rows, forward, 0)

    def mark(i, _):
        size = 128
        at = pl.ds(pl.multiple_of(i * size, size), size)
        row = lax.broadcasted_iota(jnp.int32, (size, entries), 0) + i * size
        onehot[at, :] = jnp.where(row == slot_ref[...], 1.0, 0.0).astype(BF16)
        return _

    lax.fori_loop(0, slots // 128, mark, 0)

    pl.semaphore_wait(barrier, 1 + (nd - 1) + has_above.astype(jnp.int32) + has_below.astype(jnp.int32))

    def my_rows(c):
        return pl.ds(pl.multiple_of(b * half + c * sub, sub), sub)

    def peer_rows(c):
        return pl.ds(pl.multiple_of((1 - b) * half + c * sub, sub), sub)

    def copy(src, dst, send, recv, where):
        return pltpu.make_async_remote_copy(
            src_ref=src, dst_ref=dst, send_sem=send, recv_sem=recv,
            device_id=where, device_id_type=MESH,
        )

    def f_copy(t, c):
        return copy(fsend.at[t, c], frecv.at[t, c], fs_sem.at[t, c], fr_sem.at[t, c], peer)

    def z_copy(way, t, c):
        return copy(
            zsend.at[t, c], zrecv.at[way, t, c], zs_sem.at[t, c], zr_sem.at[way, t, c],
            below if way else above,
        )

    def g_copy(way, t, c):
        block = resid.at[t, my_rows(c)]
        return copy(
            block, block, gs_sem.at[way, t, c], gr_sem.at[way, t, c], below if way else above
        )

    def p_copy(t, c, arriving=False):
        block = resid.at[t, peer_rows(c) if arriving else my_rows(c)]
        return copy(block, block, ps_sem.at[t, c], pr_sem.at[t, c], peer)

    def scatter(t, c):
        tile = jnp.broadcast_to(cols[:, 0:1], (entries, pixels))
        masked[...] = jnp.where(tile == t, traces[...].astype(F32), 0.0).astype(BF16)
        fsend[t, c] = dot(onehot[peer_rows(c), :], masked[...]).astype(BF16)
        f_copy(t, c).start()
        own[t, c] = dot(onehot[my_rows(c), :], masked[...])

    def up_tile(s):
        return n - 1 - s + z

    def down_tile(s):
        return s - (n - 1 - z)

    def both(s, act):
        pl.when(s >= z)(lambda: act(0, up_tile(s)))
        pl.when(s >= n - 1 - z)(lambda: act(1, down_tile(s)))

    def scatter_step(s, c):
        both(s, lambda way, t: scatter(t, c))

    def take(way, t, c):
        def go():
            z_copy(way, t, c).wait_recv()
            own[t, c] = own[t, c] + zrecv[way, t, c].astype(F32)

        pl.when(has_above if way else has_below)(go)

    def reduce_step(s, c):
        def act(way, t):
            f_copy(t, c).wait_recv()
            own[t, c] = own[t, c] + frecv[t, c].astype(F32)
            take(way, t, c)
            zsend[t, c] = own[t, c].astype(BF16)
            z_copy(way, t, c).start()

        both(s, act)

    def pass_on(way, t, c):
        pl.when(has_below if way else has_above)(lambda: g_copy(way, t, c).start())

    def finish(c):
        f_copy(z, c).wait_recv()
        own[z, c] = own[z, c] + frecv[z, c].astype(F32)
        take(0, z, c)
        take(1, z, c)
        at = my_rows(c)
        out = bad_ref[at, :].astype(F32) * (own[z, c] - obs_ref[at, :].astype(F32))
        resid[z, at, :] = out.astype(BF16)
        pass_on(0, z, c)
        pass_on(1, z, c)
        p_copy(z, c).start()

    def around(s, act):
        pl.when(z - s >= 0)(lambda: act(0, z - s))
        pl.when(z + s <= n - 1)(lambda: act(1, z + s))

    def gather_step(s, c):
        def act(way, t):
            g_copy(way, t, c).wait_recv()
            pass_on(way, t, c)
            p_copy(t, c).start()

        around(s, act)

    def use(t, c):
        p_copy(t, c, arriving=True).wait_recv()

        def block(i, _):
            at = pl.ds(pl.multiple_of(i * step_rows, step_rows), step_rows)
            got = dot(onehot_t[at, my_rows(c)], resid[t, my_rows(c), :])
            got = got + dot(onehot_t[at, peer_rows(c)], resid[t, peer_rows(c), :])
            tile = jnp.broadcast_to(cols[at, 0:1], (step_rows, pixels))
            rows[at, :] = rows[at, :] + jnp.where(tile == t, got, 0.0)
            return _

        lax.fori_loop(0, entries // step_rows, block, 0)

    def loop(first, last, act):
        def body(s, _):
            act(s)
            return _

        lax.fori_loop(first, last, body, 0)

    loop(0, n - 1, lambda s: scatter_step(s, 0))
    reduce_step(0, 0)
    scatter(z, 0)

    rows[...] = jnp.zeros_like(rows)

    def turn(k, _):
        at = pl.ds(pl.multiple_of(k * pixels, pixels), pixels)
        psf_t[at, :] = psf_ref[k].T
        return _

    lax.fori_loop(0, kinds, turn, 0)

    def mark_t(i, _):
        size = 128
        at = pl.ds(pl.multiple_of(i * size, size), size)
        lane = lax.broadcasted_iota(jnp.int32, (size, slots), 1)
        onehot_t[at, :] = jnp.where(lane == cols[at, 1:2], 1.0, 0.0).astype(BF16)
        return _

    lax.fori_loop(0, entries // 128, mark_t, 0)

    def phase_first(s):
        reduce_step(s, 0)
        if parts > 1:
            scatter_step(s - 1, 1)

    loop(1, n - 1, phase_first)
    if parts > 1:
        scatter_step(n - 2, 1)
        scatter(z, 1)
    finish(0)

    for c in range(1, parts + 1):
        reducing = c < parts

        def phase(s):
            if reducing:
                reduce_step(s - 1, c)
            gather_step(s, c - 1)

            def earlier():
                if reducing and c + 1 < parts:
                    scatter_step(s - 1, c + 1)

            earlier()
            pl.when(s == 1)(lambda: use(z, c - 1))
            pl.when(s > 1)(lambda: around(s - 1, lambda way, t: use(t, c - 1)))

        loop(1, n, phase)
        if reducing:
            if c + 1 < parts:
                scatter(z, c + 1)
            finish(c)
        around(n - 1, lambda way, t: use(t, c - 1))

    res_ref[...] = resid[z]

    def backward(i, _):
        at = pl.ds(pl.multiple_of(i * step_rows, step_rows), step_rows)
        col = cols[at, :]
        kind = jnp.broadcast_to(col[:, 4:5], (step_rows, pixels))
        term = dot(spread(rows[at, :], kind, kinds), psf_t[...])
        block = jnp.broadcast_to(col[:, 3:4], (step_rows, bins))
        terms[at, :] = spread(term, block, blocks)
        return _

    lax.fori_loop(0, entries // step_rows, backward, 0)

    share = sources // nd

    def summed(to):
        row = lax.broadcasted_iota(jnp.int32, (share, entries), 0) + to * share
        member = jnp.where(row == src_ref[...], 1.0, 0.0).astype(BF16)
        return dot(member, terms[...])

    def d_copy(k):
        to = lax.rem(d + k, nd)
        return copy(
            dsend.at[k - 1], drecv.at[k - 1], ds_sem.at[k - 1], dr_sem.at[k - 1], {"dither": to}
        )

    for k in range(1, nd):
        dsend[k - 1] = summed(lax.rem(d + k, nd)).astype(BF16)
        d_copy(k).start()
    grad_ref[...] = summed(d)
    for k in range(1, nd):
        d_copy(k).wait_recv()
        grad_ref[...] = grad_ref[...] + drecv[k - 1].astype(F32)
        d_copy(k).wait_send()

    for c in range(parts):
        loop(0, n, lambda t: f_copy(t, c).wait_send())
        loop(0, n - 1, lambda s: both(s, lambda way, t: z_copy(way, t, c).wait_send()))

        def sent(way, t):
            pl.when(has_below if way else has_above)(lambda: g_copy(way, t, c).wait_send())

        sent(0, z)
        sent(1, z)
        loop(1, n, lambda s: around(s, sent))
        loop(0, n, lambda t: p_copy(t, c).wait_send())


def per_device(
    n, nd, spectra, psf_blocks, observed, bad_mask,
    trace_tile, trace_slot, trace_source, trace_block, psf_index,
):
    entries = trace_slot.shape[0]
    slots, pixels = observed.shape[1:]
    kinds, bins, _ = psf_blocks.shape
    sources, wide = spectra.shape
    parts = 2
    sub = slots // 2 // parts
    row = lambda a: a.reshape(1, entries)
    dma = pltpu.SemaphoreType.DMA
    grad, res = pl.pallas_call(
        functools.partial(kernel, (n, nd, parts, sub)),
        out_shape=(
            jax.ShapeDtypeStruct((sources // nd, wide), F32),
            jax.ShapeDtypeStruct((slots, pixels), BF16),
        ),
        in_specs=[pl.BlockSpec(memory_space=pltpu.VMEM)] * 9,
        out_specs=[pl.BlockSpec(memory_space=pltpu.VMEM)] * 2,
        scratch_shapes=[
            pltpu.VMEM((entries, 8), jnp.int32),
            pltpu.VMEM((entries, pixels), BF16),
            pltpu.VMEM((entries, pixels), BF16),
            pltpu.VMEM((slots, entries), BF16),
            pltpu.VMEM((entries, slots), BF16),
            pltpu.VMEM((kinds * pixels, bins), BF16),
            pltpu.VMEM((n, parts, sub, pixels), F32),
            pltpu.VMEM((n, parts, sub, pixels), BF16),
            pltpu.VMEM((n, parts, sub, pixels), BF16),
            pltpu.VMEM((2, n, parts, sub, pixels), BF16),
            pltpu.VMEM((n, parts, sub, pixels), BF16),
            pltpu.VMEM((n, slots, pixels), BF16),
            pltpu.VMEM((entries, pixels), F32),
            pltpu.VMEM((entries, wide), BF16),
            pltpu.VMEM((nd - 1, sources // nd, wide), BF16),
            pltpu.VMEM((nd - 1, sources // nd, wide), BF16),
            dma((n, parts)), dma((n, parts)),
            dma((n, parts)), dma((2, n, parts)),
            dma((2, n, parts)), dma((2, n, parts)),
            dma((n, parts)), dma((n, parts)),
            dma((nd - 1,)), dma((nd - 1,)),
        ],
        compiler_params=pltpu.CompilerParams(
            collective_id=0, has_side_effects=True, vmem_limit_bytes=56 * 1024 * 1024
        ),
        cost_estimate=pl.CostEstimate(
            flops=2 * entries * pixels * (2 * kinds * bins + 2 * n * slots + 8 * sources),
            bytes_accessed=2 * 1024 * 1024,
            transcendentals=0,
        ),
    )(
        spectra, psf_blocks, observed[0], bad_mask[0],
        row(trace_tile), row(trace_slot), row(trace_source), row(trace_block), row(psf_index),
    )
    return grad, res[None]


def solution(mesh):
    in_specs = (
        P(("groups", "tile"), "band"),
        P(),
        P(("groups", "dither"), "tile", None),
        P(("groups", "dither"), "tile", None),
        P(("groups", "tile", "dither", "band"), None),
        P(("groups", "tile", "dither", "band")),
        P(("groups", "tile", "dither", "band"), None),
        P(("groups", "tile", "dither", "band")),
        P(("groups", "tile", "dither", "band")),
    )
    out_specs = (P(("groups", "tile", "dither"), "band"), P(("groups", "dither"), "tile", None))
    fn = functools.partial(per_device, mesh.shape["tile"], mesh.shape["dither"])
    return jax.shard_map(fn, mesh=mesh, in_specs=in_specs, out_specs=out_specs, check_vma=False)
```

time: 172 us -> 56.5 us (0.33)
  Pallas kernels: 0 us -> 53.2 us
  other arithmetic: 44.5 us -> 0 us
  waiting for transfers between devices: 43.6 us -> 0 us
  local copies, waits for them, and re-layouts: 25.9 us -> 2.42 us
  blocking collectives: 19.6 us -> 0 us
  starting transfers between devices: 14.7 us -> 0 us
  between operations: 14.2 us -> 0.65 us
  matrix products: 9.29 us -> 0 us
    pallas_call x0 -> x1, Pallas kernels: none -> 53.2 us  [per_device(): pl.pallas_call(functools.partial(kernel, (n, nd, parts, sub)), out_shape=...]
    scatter-add x2 -> x0, other arithmetic: 25.5 us -> none  [the longest x1 13.9 us: per_device(): jax.ops.segment_sum(flat_traces.astype(jnp.float32), flat_slots, slot_count)]
    psum x1 -> x0, waiting for transfers between devices: 21 us -> none  [per_device(): model_image = lax.psum(partial_value, 'band')]
    all_to_all x1 -> x0, blocking collectives: 19.6 us -> none  [per_device(): lax.all_to_all(owner_terms.reshape(tile_count, capacity, bin_count).astyp...]
    unnamed x12 -> x4, local copies, waits for them, and re-layouts: 17.2 us -> 2.42 us
    all_to_all x3 -> x0, starting transfers between devices: 14.7 us -> none  [the longest x1 6.32 us: per_device(): lax.all_to_all(send_kinds, 'tile', split_axis=0, concat_axis=0, tiled=True)]
    reduce_scatter x1 -> x0, waiting for transfers between devices: 13.7 us -> none  [per_device(): lax.psum_scatter(local_grad, 'dither', scatter_dimension=0, tiled=True)]
    select_n x5 -> x0, other arithmetic: 10.8 us -> none  [the longest x4 10.8 us: through_single(): jnp.where(chosen, part_values[:, None, :], jnp.zeros((), jnp.bfloat16))]
  transfers between devices with their start and end apart: 5 -> 0, of which waited for: 3 -> 0; matrix products, arithmetic and copies ran while one was open for 16% -> 0% of each run, Pallas kernels for 0% -> 0%
where the time goes in v1:
time: 56.5 us; the launch traced here: 56.3 us
  Pallas kernels  53.2 us (94%)
  local copies, waits for them, and re-layouts  2.42 us (4%)
  between operations  0.65 us (1%)
    pallas_call x1, Pallas kernels, per_device(): pl.pallas_call(functools.partial(kernel, (n, nd, parts, sub)), out_shape=...  53.2 us
    unnamed x4, local copies, waits for them, and re-layouts  2.42 us

profile of v1, /device:TPU:0, one launch (start us, length us, event | category | flops | bytes accessed | tf_op | source)
XLA Modules:
  0.0 56.3 jit_solution(7734354085290381231)
XLA Ops:
  0.6 53.2 %shard_map.104 = (f32[128,512]{1,0:T(8,128)}, bf16[1024,128]{1,0:T(8,128)(2,1)}) custom-call(bf16[256,512]{1,0:T(8,128)(2,1)} %spectra_ref.1, bf16[16,128,128]{2,1,0:T(8,128)(2,1)} %psf_ref.1, bf16[1024,128]{1,0:T(8,128)(2,1)} %bitcast.10, s32[1024,128]{1,0:T(8,128)} %bitcast.9, s32[1,1024]{1,0:T(1,128)} %bitcast.11, s32[1,1024]{1,0:T(1,128)} %bitcast.12, ...), custom_call_target="tpu_custom_call" | custom-call | flops 3758096384 | bytes 2097152 | tf_op jit(solution)/shard_map/pallas_call | solution.py:319
  53.9 0.0 copy-start
  53.9 1.7 %copy.13 = f32[128,512]{1,0:T(8,128)} copy(f32[128,512]{1,0:T(8,128)} %get-tuple-element.8) | data formatting | bytes 524288
  55.6 0.0 copy-done
  55.6 0.7 %copy.14 = bf16[1,1024,128]{2,1,0:T(8,128)(2,1)} copy(bf16[1,1024,128]{2,1,0:T(8,128)(2,1)S(1)} %bitcast.8) | data formatting | bytes 524288
Async XLA Ops:
  53.9 1.7 %copy-start = (bf16[1024,128]{1,0:T(8,128)(2,1)S(1)}, bf16[1024,128]{1,0:T(8,128)(2,1)}, u32[]{:S(2)}) copy-start(bf16[1024,128]{1,0:T(8,128)(2,1)} %get-tuple-element.5) | copy-start | bytes 786436

commit v2 on v1

--- a/solution.py
+++ b/solution.py
@@ -19,7 +19,7 @@
     cfg,
     spectra_ref, psf_ref, obs_ref, bad_ref, tile_ref, slot_ref, src_ref, blk_ref, kind_ref,
     grad_ref, res_ref,
-    cols, traces, masked, onehot, onehot_t, psf_t, own, fsend, frecv, zrecv, zsend,
+    cols, traces, masked, onehot, onehot_t, psf_f, psf_t, own, fsend, frecv, zrecv, zsend,
     resid, rows, terms, dsend, drecv,
     fs_sem, fr_sem, zs_sem, zr_sem, gs_sem, gr_sem, ps_sem, pr_sem, ds_sem, dr_sem,
 ):
@@ -30,6 +30,7 @@
     kinds, bins, pixels = psf_ref.shape
     sources, wide = spectra_ref.shape
     blocks = wide // bins
+    fold = kinds // 2
     step_rows = min(256, entries)
     z = lax.axis_index("tile")
     b = lax.axis_index("band")
@@ -56,6 +57,16 @@
         return jnp.concatenate(
             [jnp.where(which == k, values, 0.0).astype(BF16) for k in range(count)], axis=1
         )
+
+    def through(values, kind, table):
+        low = kind < fold
+        product = dot(spread(values, jnp.where(low, kind, kind - fold), fold), table[...])
+        width = product.shape[1] // 2
+        return jnp.where(low, product[:, :width], product[:, width:])
+
+    flat = psf_ref[...].reshape(kinds * bins, pixels)
+    psf_f[:, 0:pixels] = flat[:fold * bins]
+    psf_f[:, pixels:2 * pixels] = flat[fold * bins:]
 
     def forward(i, _):
         at = pl.ds(pl.multiple_of(i * step_rows, step_rows), step_rows)
@@ -68,8 +79,7 @@
         for k in range(blocks):
             value = jnp.where(block == k, found[:, k * bins:(k + 1) * bins], value)
         kind = jnp.broadcast_to(col[:, 4:5], (step_rows, bins))
-        table = psf_ref[...].reshape(kinds * bins, pixels)
-        traces[at, :] = dot(spread(value, kind, kinds), table).astype(BF16)
+        traces[at, :] = through(value, kind, psf_f).astype(BF16)
         return _
 
     lax.fori_loop(0, entries // step_rows, forward, 0)
@@ -200,61 +210,65 @@
 
         lax.fori_loop(first, last, body, 0)
 
-    loop(0, n - 1, lambda s: scatter_step(s, 0))
-    reduce_step(0, 0)
-    scatter(z, 0)
-
-    rows[...] = jnp.zeros_like(rows)
-
-    def turn(k, _):
-        at = pl.ds(pl.multiple_of(k * pixels, pixels), pixels)
-        psf_t[at, :] = psf_ref[k].T
-        return _
-
-    lax.fori_loop(0, kinds, turn, 0)
-
-    def mark_t(i, _):
-        size = 128
-        at = pl.ds(pl.multiple_of(i * size, size), size)
-        lane = lax.broadcasted_iota(jnp.int32, (size, slots), 1)
-        onehot_t[at, :] = jnp.where(lane == cols[at, 1:2], 1.0, 0.0).astype(BF16)
-        return _
-
-    lax.fori_loop(0, entries // 128, mark_t, 0)
-
-    def phase_first(s):
-        reduce_step(s, 0)
-        if parts > 1:
-            scatter_step(s - 1, 1)
-
-    loop(1, n - 1, phase_first)
-    if parts > 1:
-        scatter_step(n - 2, 1)
-        scatter(z, 1)
-    finish(0)
-
-    for c in range(1, parts + 1):
-        reducing = c < parts
+    def prepare():
+        rows[...] = jnp.zeros_like(rows)
+
+        def turn(k, _):
+            at = pl.ds(pl.multiple_of(k * pixels, pixels), pixels)
+            psf_t[at, 0:bins] = psf_ref[k].T
+            psf_t[at, bins:2 * bins] = psf_ref[k + fold].T
+            return _
+
+        lax.fori_loop(0, fold, turn, 0)
+
+        def mark_t(i, _):
+            size = 128
+            at = pl.ds(pl.multiple_of(i * size, size), size)
+            lane = lax.broadcasted_iota(jnp.int32, (size, slots), 1)
+            onehot_t[at, :] = jnp.where(lane == cols[at, 1:2], 1.0, 0.0).astype(BF16)
+            return _
+
+        lax.fori_loop(0, entries // 128, mark_t, 0)
+
+    middle = has_above & has_below
+
+    def use_around(s, c):
+        around(s, lambda way, t: use(t, c))
+
+    def scatter_after(s, c):
+        pl.when(s < n - 2)(lambda: scatter_step(s + 1, c))
+        pl.when(s == n - 2)(lambda: scatter(z, c))
+
+    for c in range(parts + 1):
+        if c < parts:
+            scatter_step(0, c)
+            scatter_after(0, c)
+            reduce_step(0, c)
+        if c == 0:
+            pl.when(middle)(prepare)
+        if c == 1:
+            pl.when(jnp.logical_not(middle))(prepare)
+        if c >= 2:
+            gather_step(n - 1, c - 2)
+        if c >= 1:
+            finish(c - 1)
+        if c >= 2:
+            use_around(n - 2, c - 2)
+            use_around(n - 1, c - 2)
 
         def phase(s):
-            if reducing:
-                reduce_step(s - 1, c)
-            gather_step(s, c - 1)
-
-            def earlier():
-                if reducing and c + 1 < parts:
-                    scatter_step(s - 1, c + 1)
-
-            earlier()
-            pl.when(s == 1)(lambda: use(z, c - 1))
-            pl.when(s > 1)(lambda: around(s - 1, lambda way, t: use(t, c - 1)))
-
-        loop(1, n, phase)
-        if reducing:
-            if c + 1 < parts:
-                scatter(z, c + 1)
-            finish(c)
-        around(n - 1, lambda way, t: use(t, c - 1))
+            if c < parts:
+                scatter_after(s, c)
+                reduce_step(s, c)
+            if c >= 1:
+                gather_step(s, c - 1)
+                pl.when(s == 1)(lambda: use(z, c - 1))
+                pl.when(s > 1)(lambda: use_around(s - 1, c - 1))
+
+        loop(1, n - 1, phase)
+    gather_step(n - 1, parts - 1)
+    use_around(n - 2, parts - 1)
+    use_around(n - 1, parts - 1)
 
     res_ref[...] = resid[z]
 
@@ -262,7 +276,7 @@
         at = pl.ds(pl.multiple_of(i * step_rows, step_rows), step_rows)
         col = cols[at, :]
         kind = jnp.broadcast_to(col[:, 4:5], (step_rows, pixels))
-        term = dot(spread(rows[at, :], kind, kinds), psf_t[...])
+        term = through(rows[at, :], kind, psf_t)
         block = jnp.broadcast_to(col[:, 3:4], (step_rows, bins))
         terms[at, :] = spread(term, block, blocks)
         return _
@@ -330,7 +344,8 @@
             pltpu.VMEM((entries, pixels), BF16),
             pltpu.VMEM((slots, entries), BF16),
             pltpu.VMEM((entries, slots), BF16),
-            pltpu.VMEM((kinds * pixels, bins), BF16),
+            pltpu.VMEM((kinds // 2 * bins, 2 * pixels), BF16),
+            pltpu.VMEM((kinds // 2 * pixels, 2 * bins), BF16),
             pltpu.VMEM((n, parts, sub, pixels), F32),
             pltpu.VMEM((n, parts, sub, pixels), BF16),
             pltpu.VMEM((n, parts, sub, pixels), BF16),

time: 56.5 us -> 54.1 us (0.958)
  Pallas kernels: 53.2 us -> 50.9 us
    pallas_call x1, Pallas kernels: 53.2 us -> 50.9 us  [per_device(): pl.pallas_call(functools.partial(kernel, (n, nd, parts, sub)), out_shape=...]
where the time goes in v2:
time: 54.1 us; the launch traced here: 54 us
  Pallas kernels  50.9 us (94%)
  local copies, waits for them, and re-layouts  2.42 us (4%)
  between operations  0.65 us (1%)
    pallas_call x1, Pallas kernels, per_device(): pl.pallas_call(functools.partial(kernel, (n, nd, parts, sub)), out_shape=...  50.9 us
    unnamed x4, local copies, waits for them, and re-layouts  2.42 us

profile of v2, /device:TPU:0, one launch (start us, length us, event | category | flops | bytes accessed | tf_op | source)
XLA Modules:
  0.0 54.0 jit_solution(9588333741852028705)
XLA Ops:
  0.6 50.9 %shard_map.104 = (f32[128,512]{1,0:T(8,128)}, bf16[1024,128]{1,0:T(8,128)(2,1)}) custom-call(bf16[256,512]{1,0:T(8,128)(2,1)} %spectra_ref.1, bf16[16,128,128]{2,1,0:T(8,128)(2,1)} %psf_ref.1, bf16[1024,128]{1,0:T(8,128)(2,1)} %bitcast.10, s32[1024,128]{1,0:T(8,128)} %bitcast.9, s32[1,1024]{1,0:T(1,128)} %bitcast.11, s32[1,1024]{1,0:T(1,128)} %bitcast.12, ...), custom_call_target="tpu_custom_call" | custom-call | flops 3758096384 | bytes 2097152 | tf_op jit(solution)/shard_map/pallas_call | solution.py:333
  51.5 0.0 copy-start
  51.5 1.7 %copy.13 = f32[128,512]{1,0:T(8,128)} copy(f32[128,512]{1,0:T(8,128)} %get-tuple-element.8) | data formatting | bytes 524288
  53.3 0.0 copy-done
  53.3 0.7 %copy.14 = bf16[1,1024,128]{2,1,0:T(8,128)(2,1)} copy(bf16[1,1024,128]{2,1,0:T(8,128)(2,1)S(1)} %bitcast.8) | data formatting | bytes 524288
Async XLA Ops:
  51.5 1.7 %copy-start = (bf16[1024,128]{1,0:T(8,128)(2,1)S(1)}, bf16[1024,128]{1,0:T(8,128)(2,1)}, u32[]{:S(2)}) copy-start(bf16[1024,128]{1,0:T(8,128)(2,1)} %get-tuple-element.5) | copy-start | bytes 786436

commit v3 on v2

--- a/solution.py
+++ b/solution.py
@@ -326,7 +326,7 @@
     slots, pixels = observed.shape[1:]
     kinds, bins, _ = psf_blocks.shape
     sources, wide = spectra.shape
-    parts = 2
+    parts = 1
     sub = slots // 2 // parts
     row = lambda a: a.reshape(1, entries)
     dma = pltpu.SemaphoreType.DMA

time: 54.1 us -> 50.9 us (0.941)
  Pallas kernels: 50.9 us -> 47.7 us
    pallas_call x1, Pallas kernels: 50.9 us -> 47.7 us  [per_device(): pl.pallas_call(functools.partial(kernel, (n, nd, parts, sub)), out_shape=...]
where the time goes in v3:
time: 50.9 us; the launch traced here: 50.8 us
  Pallas kernels  47.7 us (94%)
  local copies, waits for them, and re-layouts  2.42 us (5%)
  between operations  0.65 us (1%)
    pallas_call x1, Pallas kernels, per_device(): pl.pallas_call(functools.partial(kernel, (n, nd, parts, sub)), out_shape=...  47.7 us
    unnamed x4, local copies, waits for them, and re-layouts  2.42 us

profile of v3, /device:TPU:0, one launch (start us, length us, event | category | flops | bytes accessed | tf_op | source)
XLA Modules:
  0.0 50.8 jit_solution(3081272791369542788)
XLA Ops:
  0.6 47.7 %shard_map.104 = (f32[128,512]{1,0:T(8,128)}, bf16[1024,128]{1,0:T(8,128)(2,1)}) custom-call(bf16[256,512]{1,0:T(8,128)(2,1)} %spectra_ref.1, bf16[16,128,128]{2,1,0:T(8,128)(2,1)} %psf_ref.1, bf16[1024,128]{1,0:T(8,128)(2,1)} %bitcast.10, s32[1024,128]{1,0:T(8,128)} %bitcast.9, s32[1,1024]{1,0:T(1,128)} %bitcast.11, s32[1,1024]{1,0:T(1,128)} %bitcast.12, ...), custom_call_target="tpu_custom_call" | custom-call | flops 3758096384 | bytes 2097152 | tf_op jit(solution)/shard_map/pallas_call | solution.py:333
  48.3 0.0 copy-start
  48.3 1.7 %copy.13 = f32[128,512]{1,0:T(8,128)} copy(f32[128,512]{1,0:T(8,128)} %get-tuple-element.8) | data formatting | bytes 524288
  50.1 0.0 copy-done
  50.1 0.7 %copy.14 = bf16[1,1024,128]{2,1,0:T(8,128)(2,1)} copy(bf16[1,1024,128]{2,1,0:T(8,128)(2,1)S(1)} %bitcast.8) | data formatting | bytes 524288
Async XLA Ops:
  48.3 1.7 %copy-start = (bf16[1024,128]{1,0:T(8,128)(2,1)S(1)}, bf16[1024,128]{1,0:T(8,128)(2,1)}, u32[]{:S(2)}) copy-start(bf16[1024,128]{1,0:T(8,128)(2,1)} %get-tuple-element.5) | copy-start | bytes 786436

commit v4 on v3

v4 whole, which is shorter than its diff:
```python
import functools

import jax
import jax.numpy as jnp
from jax import lax
from jax.experimental import pallas as pl
from jax.experimental.pallas import tpu as pltpu
from jax.sharding import PartitionSpec as P

MESH = pl.DeviceIdType.MESH
F32, BF16 = jnp.float32, jnp.bfloat16


def dot(a, b):
    return jnp.dot(a, b, preferred_element_type=F32)


def kernel(
    cfg,
    spectra_ref, psf_ref, obs_ref, bad_ref, tile_ref, slot_ref, src_ref, blk_ref, kind_ref,
    grad_ref, res_ref,
    cols, traces, masked, onehot, onehot_t, psf_f, psf_t, own, fsend, frecv, zrecv, zsend,
    resid, rows, terms, dsend, drecv,
    fs_sem, fr_sem, zs_sem, zr_sem, gs_sem, gr_sem, ps_sem, pr_sem, ds_sem, dr_sem,
):
    n, nd, steps = cfg
    entries = tile_ref.shape[1]
    slots = obs_ref.shape[0]
    half = slots // 2
    kinds, bins, pixels = psf_ref.shape
    sources, wide = spectra_ref.shape
    blocks = wide // bins
    fold = kinds // 2
    step_rows = min(256, entries, half)
    z = lax.axis_index("tile")
    b = lax.axis_index("band")
    d = lax.axis_index("dither")
    peer = {"band": 1 - b}

    def bit(k):
        return lax.rem(z // (1 << k), 2)

    def partner(k):
        return {"tile": z + (1 - 2 * bit(k)) * (1 << k)}

    def kept(k, h):
        return h * (2 << k) + lax.rem(z, 2 << k)

    def other(k, h):
        return h * (2 << k) + (1 - bit(k)) * (1 << k) + lax.rem(z, 1 << k)

    barrier = pltpu.get_barrier_semaphore()

    def greet(where):
        pl.semaphore_signal(barrier, inc=1, device_id=where, device_id_type=MESH)

    greet(peer)
    for k in range(steps):
        greet(partner(k))
    for k in range(1, nd):
        greet({"dither": lax.rem(d + k, nd)})

    def loop(count, act, unroll=False):
        def body(s, _):
            act(s)
            return _

        lax.fori_loop(0, count, body, 0, unroll=unroll)

    def span(i, size, base=0):
        return pl.ds(pl.multiple_of(base + i * size, size), size)

    stack = [tile_ref[...], slot_ref[...], src_ref[...], blk_ref[...], kind_ref[...]]
    cols[...] = jnp.concatenate(stack + [kind_ref[...]] * 3, axis=0).T

    def spread(values, which, count):
        return jnp.concatenate(
            [jnp.where(which == k, values, 0.0).astype(BF16) for k in range(count)], axis=1
        )

    def through(values, kind, table):
        low = kind < fold
        product = dot(spread(values, jnp.where(low, kind, kind - fold), fold), table[...])
        width = product.shape[1] // 2
        return jnp.where(low, product[:, :width], product[:, width:])

    flat = psf_ref[...].reshape(kinds * bins, pixels)
    psf_f[:, 0:pixels] = flat[:fold * bins]
    psf_f[:, pixels:2 * pixels] = flat[fold * bins:]

    def forward(i):
        at = span(i, step_rows)
        col = cols[at, :]
        lane = lax.broadcasted_iota(jnp.int32, (step_rows, sources), 1)
        pick = jnp.where(lane == col[:, 2:3], 1.0, 0.0).astype(BF16)
        found = dot(pick, spectra_ref[...])
        block = jnp.broadcast_to(col[:, 3:4], (step_rows, bins))
        value = jnp.zeros((step_rows, bins), F32)
        for k in range(blocks):
            value = jnp.where(block == k, found[:, k * bins:(k + 1) * bins], value)
        kind = jnp.broadcast_to(col[:, 4:5], (step_rows, bins))
        traces[at, :] = through(value, kind, psf_f).astype(BF16)

    loop(entries // step_rows, forward, unroll=True)

    def mark(i):
        size = 128
        row = lax.broadcasted_iota(jnp.int32, (size, entries), 0) + i * size
        onehot[span(i, size), :] = jnp.where(row == slot_ref[...], 1.0, 0.0).astype(BF16)

    loop(slots // 128, mark)

    pl.semaphore_wait(barrier, 1 + steps + nd - 1)

    mine, theirs = span(b, half), span(1 - b, half)

    def copy(src, dst, send, recv, where):
        return pltpu.make_async_remote_copy(
            src_ref=src, dst_ref=dst, send_sem=send, recv_sem=recv,
            device_id=where, device_id_type=MESH,
        )

    def f_copy(t):
        return copy(fsend.at[t], frecv.at[t], fs_sem.at[t], fr_sem.at[t], peer)

    def z_copy(k, h):
        t = other(k, h)
        return copy(zsend.at[t], zrecv.at[k, h], zs_sem.at[t], zr_sem.at[k, h], partner(k))

    def g_copy(k, h):
        block = resid.at[kept(k, h), mine]
        return copy(block, block, gs_sem.at[k, h], gr_sem.at[k, h], partner(k))

    def p_copy(t, arriving=False):
        block = resid.at[t, theirs if arriving else mine]
        return copy(block, block, ps_sem.at[t], pr_sem.at[t], peer)

    def scatter(t, u):
        tile = jnp.broadcast_to(cols[:, 0:1], (entries, pixels))
        trace = traces[...].astype(F32)
        masked[:, 0:pixels] = jnp.where(tile == t, trace, 0.0).astype(BF16)
        masked[:, pixels:2 * pixels] = jnp.where(tile == u, trace, 0.0).astype(BF16)

        def away(i):
            part = dot(onehot[span(i, step_rows, (1 - b) * half), :], masked[...]).astype(BF16)
            fsend[t, span(i, step_rows), :] = part[:, 0:pixels]
            fsend[u, span(i, step_rows), :] = part[:, pixels:2 * pixels]

        loop(half // step_rows, away, unroll=True)
        f_copy(t).start()
        f_copy(u).start()

        def here(i):
            part = dot(onehot[span(i, step_rows, b * half), :], masked[...])
            own[t, span(i, step_rows), :] = part[:, 0:pixels]
            own[u, span(i, step_rows), :] = part[:, pixels:2 * pixels]

        loop(half // step_rows, here, unroll=True)

    def total(t, k):
        f_copy(t).wait_recv()
        value = own[t] + frecv[t].astype(F32)
        for j in range(k):
            z_copy(j, t // (2 << j)).wait_recv()
            value = value + zrecv[j, t // (2 << j)].astype(F32)
        return value

    loop(n // 4, lambda j: scatter(other(0, 2 * j), other(0, 2 * j + 1)))
    loop(n // 4, lambda j: scatter(kept(0, 2 * j), kept(0, 2 * j + 1)))

    def reduce_step(k):
        count = n >> (k + 1)

        def send(i):
            h = lax.rem(z // (2 << k) + i + count // 2, count)
            t = other(k, h)
            zsend[t] = total(t, k).astype(BF16)
            z_copy(k, h).start()

        loop(count, send)

    reduce_step(0)

    rows[...] = jnp.zeros_like(rows)

    def turn(k):
        psf_t[span(k, pixels), 0:bins] = psf_ref[k].T
        psf_t[span(k, pixels), bins:2 * bins] = psf_ref[k + fold].T

    loop(fold, turn)

    def mark_t(i):
        size = 128
        lane = lax.broadcasted_iota(jnp.int32, (size, slots), 1)
        slot = cols[span(i, size), 1:2]
        onehot_t[span(i, size), :] = jnp.where(lane == slot, 1.0, 0.0).astype(BF16)

    loop(entries // 128, mark_t)

    for k in range(1, steps):
        reduce_step(k)
    model = total(z, steps)
    out = bad_ref[mine, :].astype(F32) * (model - obs_ref[mine, :].astype(F32))
    resid[z, mine, :] = out.astype(BF16)

    def pass_on(t, k):
        for j in reversed(range(k)):
            g_copy(j, t // (2 << j)).start()
        p_copy(t).start()

    pass_on(z, steps)

    def use(h):
        def gathered(where):
            pair = jnp.concatenate([resid[2 * h, where, :], resid[2 * h + 1, where, :]], axis=1)

            def block(i):
                at = span(i, step_rows)
                got = dot(onehot_t[at, where], pair)
                tile = jnp.broadcast_to(cols[at, 0:1], (step_rows, pixels))
                value = jnp.where(tile == 2 * h, got[:, 0:pixels], 0.0)
                value = jnp.where(tile == 2 * h + 1, got[:, pixels:2 * pixels], value)
                rows[at, :] = rows[at, :] + value

            loop(entries // step_rows, block, unroll=True)

        gathered(mine)
        p_copy(2 * h, arriving=True).wait_recv()
        p_copy(2 * h + 1, arriving=True).wait_recv()
        gathered(theirs)

    for k in reversed(range(steps)):
        count = n >> (k + 1)

        def arrive(i):
            h = lax.rem(z // (2 << k) + i, count)
            g_copy(k, h).wait_recv()
            pass_on(other(k, h), k)
            if k == 0:
                use(h)

        loop(count, arrive)

    res_ref[...] = resid[z]

    def backward(i):
        at = span(i, step_rows)
        col = cols[at, :]
        kind = jnp.broadcast_to(col[:, 4:5], (step_rows, pixels))
        term = through(rows[at, :], kind, psf_t)
        block = jnp.broadcast_to(col[:, 3:4], (step_rows, bins))
        terms[at, :] = spread(term, block, blocks)

    loop(entries // step_rows, backward, unroll=True)

    share = sources // nd

    def summed(to):
        row = lax.broadcasted_iota(jnp.int32, (share, entries), 0) + to * share
        member = jnp.where(row == src_ref[...], 1.0, 0.0).astype(BF16)
        return dot(member, terms[...])

    def d_copy(k):
        to = lax.rem(d + k, nd)
        return copy(
            dsend.at[k - 1], drecv.at[k - 1], ds_sem.at[k - 1], dr_sem.at[k - 1], {"dither": to}
        )

    for k in range(1, nd):
        dsend[k - 1] = summed(lax.rem(d + k, nd)).astype(BF16)
        d_copy(k).start()
    grad_ref[...] = summed(d)
    for k in range(1, nd):
        d_copy(k).wait_recv()
        grad_ref[...] = grad_ref[...] + drecv[k - 1].astype(F32)
        d_copy(k).wait_send()

    loop(n, lambda t: f_copy(t).wait_send())
    loop(n, lambda t: p_copy(t).wait_send())
    for k in range(steps):
        loop(n >> (k + 1), lambda h: z_copy(k, h).wait_send())
        loop(n >> (k + 1), lambda h: g_copy(k, h).wait_send())


def per_device(
    n, nd, spectra, psf_blocks, observed, bad_mask,
    trace_tile, trace_slot, trace_source, trace_block, psf_index,
):
    entries = trace_slot.shape[0]
    slots, pixels = observed.shape[1:]
    kinds, bins, _ = psf_blocks.shape
    sources, wide = spectra.shape
    half = slots // 2
    steps = n.bit_length() - 1
    row = lambda a: a.reshape(1, entries)
    dma = pltpu.SemaphoreType.DMA
    grad, res = pl.pallas_call(
        functools.partial(kernel, (n, nd, steps)),
        out_shape=(
            jax.ShapeDtypeStruct((sources // nd, wide), F32),
            jax.ShapeDtypeStruct((slots, pixels), BF16),
        ),
        in_specs=[pl.BlockSpec(memory_space=pltpu.VMEM)] * 9,
        out_specs=[pl.BlockSpec(memory_space=pltpu.VMEM)] * 2,
        scratch_shapes=[
            pltpu.VMEM((entries, 8), jnp.int32),
            pltpu.VMEM((entries, pixels), BF16),
            pltpu.VMEM((entries, 2 * pixels), BF16),
            pltpu.VMEM((slots, entries), BF16),
            pltpu.VMEM((entries, slots), BF16),
            pltpu.VMEM((kinds // 2 * bins, 2 * pixels), BF16),
            pltpu.VMEM((kinds // 2 * pixels, 2 * bins), BF16),
            pltpu.VMEM((n, half, pixels), F32),
            pltpu.VMEM((n, half, pixels), BF16),
            pltpu.VMEM((n, half, pixels), BF16),
            pltpu.VMEM((steps, n // 2, half, pixels), BF16),
            pltpu.VMEM((n, half, pixels), BF16),
            pltpu.VMEM((n, slots, pixels), BF16),
            pltpu.VMEM((entries, pixels), F32),
            pltpu.VMEM((entries, wide), BF16),
            pltpu.VMEM((nd - 1, sources // nd, wide), BF16),
            pltpu.VMEM((nd - 1, sources // nd, wide), BF16),
            dma((n,)), dma((n,)),
            dma((n,)), dma((steps, n // 2)),
            dma((steps, n // 2)), dma((steps, n // 2)),
            dma((n,)), dma((n,)),
            dma((nd - 1,)), dma((nd - 1,)),
        ],
        compiler_params=pltpu.CompilerParams(
            collective_id=0, has_side_effects=True, vmem_limit_bytes=56 * 1024 * 1024
        ),
        cost_estimate=pl.CostEstimate(
            flops=2 * entries * pixels * (2 * kinds * bins + 2 * n * slots + 8 * sources),
            bytes_accessed=2 * 1024 * 1024,
            transcendentals=0,
        ),
    )(
        spectra, psf_blocks, observed[0], bad_mask[0],
        row(trace_tile), row(trace_slot), row(trace_source), row(trace_block), row(psf_index),
    )
    return grad, res[None]


def solution(mesh):
    in_specs = (
        P(("groups", "tile"), "band"),
        P(),
        P(("groups", "dither"), "tile", None),
        P(("groups", "dither"), "tile", None),
        P(("groups", "tile", "dither", "band"), None),
        P(("groups", "tile", "dither", "band")),
        P(("groups", "tile", "dither", "band"), None),
        P(("groups", "tile", "dither", "band")),
        P(("groups", "tile", "dither", "band")),
    )
    out_specs = (P(("groups", "tile", "dither"), "band"), P(("groups", "dither"), "tile", None))
    fn = functools.partial(per_device, mesh.shape["tile"], mesh.shape["dither"])
    return jax.shard_map(fn, mesh=mesh, in_specs=in_specs, out_specs=out_specs, check_vma=False)
```

time: 50.9 us -> 42.4 us (0.83)
  Pallas kernels: 47.7 us -> 39.1 us
    pallas_call x1, Pallas kernels: 47.7 us -> 39.1 us  [per_device(): pl.pallas_call(functools.partial(kernel, (n, nd, steps)), out_shape=(jax....]
where the time goes in v4:
time: 42.4 us; the launch traced here: 42.2 us
  Pallas kernels  39.1 us (92%)
  local copies, waits for them, and re-layouts  2.42 us (6%)
  between operations  0.65 us (2%)
    pallas_call x1, Pallas kernels, per_device(): pl.pallas_call(functools.partial(kernel, (n, nd, steps)), out_shape=(jax....  39.1 us
    unnamed x4, local copies, waits for them, and re-layouts  2.42 us

profile of v4, /device:TPU:0, one launch (start us, length us, event | category | flops | bytes accessed | tf_op | source)
XLA Modules:
  0.0 42.2 jit_solution(3121384663374109820)
XLA Ops:
  0.6 39.1 %shard_map.104 = (f32[128,512]{1,0:T(8,128)}, bf16[1024,128]{1,0:T(8,128)(2,1)}) custom-call(bf16[256,512]{1,0:T(8,128)(2,1)} %spectra_ref.1, bf16[16,128,128]{2,1,0:T(8,128)(2,1)} %psf_ref.1, bf16[1024,128]{1,0:T(8,128)(2,1)} %bitcast.10, s32[1024,128]{1,0:T(8,128)} %bitcast.9, s32[1,1024]{1,0:T(1,128)} %bitcast.11, s32[1,1024]{1,0:T(1,128)} %bitcast.12, ...), custom_call_target="tpu_custom_call" | custom-call | flops 3758096384 | bytes 2097152 | tf_op jit(solution)/shard_map/pallas_call | solution.py:297
  39.8 0.0 copy-start
  39.8 1.7 %copy.13 = f32[128,512]{1,0:T(8,128)} copy(f32[128,512]{1,0:T(8,128)} %get-tuple-element.8) | data formatting | bytes 524288
  41.5 0.0 copy-done
  41.5 0.7 %copy.14 = bf16[1,1024,128]{2,1,0:T(8,128)(2,1)} copy(bf16[1,1024,128]{2,1,0:T(8,128)(2,1)S(1)} %bitcast.8) | data formatting | bytes 524288
Async XLA Ops:
  39.8 1.7 %copy-start = (bf16[1024,128]{1,0:T(8,128)(2,1)S(1)}, bf16[1024,128]{1,0:T(8,128)(2,1)}, u32[]{:S(2)}) copy-start(bf16[1024,128]{1,0:T(8,128)(2,1)} %get-tuple-element.5) | copy-start | bytes 786436

commit v5 on v4

v5 whole, which is shorter than its diff:
```python
import functools

import jax
import jax.numpy as jnp
from jax import lax
from jax.experimental import pallas as pl
from jax.experimental.pallas import tpu as pltpu
from jax.sharding import PartitionSpec as P

MESH = pl.DeviceIdType.MESH
F32, BF16 = jnp.float32, jnp.bfloat16


def dot(a, b):
    return jnp.dot(a, b, preferred_element_type=F32)


def kernel(
    cfg,
    spectra_ref, psf_ref, obs_ref, bad_ref, tile_ref, slot_ref, src_ref, blk_ref, kind_ref,
    grad_ref, res_ref,
    cols, traces, masked, onehot, onehot_t, psf_f, psf_t, own, fsend, frecv, zrecv, zsend,
    resid, rows, terms, dsend, drecv, obs, bad,
    fs_sem, fr_sem, zs_sem, zr_sem, gs_sem, gr_sem, ps_sem, pr_sem, ds_sem, dr_sem, in_sem,
):
    n, nd, steps, parts = cfg
    entries = tile_ref.shape[1]
    slots = obs_ref.shape[0]
    half = slots // 2
    sub = half // parts
    kinds, bins, pixels = psf_ref.shape
    sources, wide = spectra_ref.shape
    blocks = wide // bins
    fold = kinds // 2
    step_rows = min(256, entries, sub)
    z = lax.axis_index("tile")
    b = lax.axis_index("band")
    d = lax.axis_index("dither")
    peer = {"band": 1 - b}

    def bit(k):
        return lax.rem(z // (1 << k), 2)

    def partner(k):
        return {"tile": z + (1 - 2 * bit(k)) * (1 << k)}

    def kept(k, h):
        return h * (2 << k) + lax.rem(z, 2 << k)

    def other(k, h):
        return h * (2 << k) + (1 - bit(k)) * (1 << k) + lax.rem(z, 1 << k)

    barrier = pltpu.get_barrier_semaphore()

    def greet(where):
        pl.semaphore_signal(barrier, inc=1, device_id=where, device_id_type=MESH)

    greet(peer)
    for k in range(steps):
        greet(partner(k))
    for k in range(1, nd):
        greet({"dither": lax.rem(d + k, nd)})

    def loop(count, act, unroll=False):
        def body(s, _):
            act(s)
            return _

        lax.fori_loop(0, count, body, 0, unroll=unroll)

    def span(i, size, base=0):
        return pl.ds(pl.multiple_of(base + i * size, size), size)

    mine, theirs = span(b, half), span(1 - b, half)
    loads = [
        pltpu.make_async_copy(obs_ref.at[mine], obs, in_sem.at[0]),
        pltpu.make_async_copy(bad_ref.at[mine], bad, in_sem.at[1]),
    ]
    for load in loads:
        load.start()

    stack = [tile_ref[...], slot_ref[...], src_ref[...], blk_ref[...], kind_ref[...]]
    cols[...] = jnp.concatenate(stack + [kind_ref[...]] * 3, axis=0).T

    def spread(values, which, count):
        return jnp.concatenate(
            [jnp.where(which == k, values, 0.0).astype(BF16) for k in range(count)], axis=1
        )

    def through(values, kind, table):
        low = kind < fold
        product = dot(spread(values, jnp.where(low, kind, kind - fold), fold), table[...])
        width = product.shape[1] // 2
        return jnp.where(low, product[:, :width], product[:, width:])

    flat = psf_ref[...].reshape(kinds * bins, pixels)
    psf_f[:, 0:pixels] = flat[:fold * bins]
    psf_f[:, pixels:2 * pixels] = flat[fold * bins:]

    def forward(i):
        at = span(i, step_rows)
        col = cols[at, :]
        lane = lax.broadcasted_iota(jnp.int32, (step_rows, sources), 1)
        pick = jnp.where(lane == col[:, 2:3], 1.0, 0.0).astype(BF16)
        found = dot(pick, spectra_ref[...])
        block = jnp.broadcast_to(col[:, 3:4], (step_rows, bins))
        value = jnp.zeros((step_rows, bins), F32)
        for k in range(blocks):
            value = jnp.where(block == k, found[:, k * bins:(k + 1) * bins], value)
        kind = jnp.broadcast_to(col[:, 4:5], (step_rows, bins))
        traces[at, :] = through(value, kind, psf_f).astype(BF16)

    loop(entries // step_rows, forward, unroll=True)

    def mark(i):
        size = 128
        row = lax.broadcasted_iota(jnp.int32, (size, entries), 0) + i * size
        onehot[span(i, size), :] = jnp.where(row == slot_ref[...], 1.0, 0.0).astype(BF16)

    loop(slots // 128, mark, unroll=True)

    pl.semaphore_wait(barrier, 1 + steps + nd - 1)

    def my_rows(c):
        return span(c, sub, b * half)

    def peer_rows(c):
        return span(c, sub, (1 - b) * half)

    def copy(src, dst, send, recv, where):
        return pltpu.make_async_remote_copy(
            src_ref=src, dst_ref=dst, send_sem=send, recv_sem=recv,
            device_id=where, device_id_type=MESH,
        )

    def f_copy(t, c):
        return copy(fsend.at[t, c], frecv.at[t, c], fs_sem.at[t, c], fr_sem.at[t, c], peer)

    def z_copy(k, h, c):
        t = other(k, h)
        return copy(
            zsend.at[t, c], zrecv.at[k, h, c], zs_sem.at[t, c], zr_sem.at[k, h, c], partner(k)
        )

    def g_copy(k, h, c):
        block = resid.at[kept(k, h), my_rows(c)]
        return copy(block, block, gs_sem.at[k, h, c], gr_sem.at[k, h, c], partner(k))

    def p_copy(t, c, arriving=False):
        block = resid.at[t, peer_rows(c) if arriving else my_rows(c)]
        return copy(block, block, ps_sem.at[t, c], pr_sem.at[t, c], peer)

    def scatter(t, u):
        tile = jnp.broadcast_to(cols[:, 0:1], (entries, pixels))
        trace = traces[...].astype(F32)
        masked[:, 0:pixels] = jnp.where(tile == t, trace, 0.0).astype(BF16)
        masked[:, pixels:2 * pixels] = jnp.where(tile == u, trace, 0.0).astype(BF16)

        for c in range(parts):
            def away(i):
                at = span(i, step_rows, (1 - b) * half + c * sub)
                part = dot(onehot[at, :], masked[...]).astype(BF16)
                fsend[t, c, span(i, step_rows), :] = part[:, 0:pixels]
                fsend[u, c, span(i, step_rows), :] = part[:, pixels:2 * pixels]

            loop(sub // step_rows, away, unroll=True)
            f_copy(t, c).start()
            f_copy(u, c).start()
        for c in range(parts):
            def here(i):
                part = dot(onehot[span(i, step_rows, b * half + c * sub), :], masked[...])
                own[t, c, span(i, step_rows), :] = part[:, 0:pixels]
                own[u, c, span(i, step_rows), :] = part[:, pixels:2 * pixels]

            loop(sub // step_rows, here, unroll=True)

    def total(t, k, c):
        f_copy(t, c).wait_recv()
        value = own[t, c] + frecv[t, c].astype(F32)
        for j in range(k):
            z_copy(j, t // (2 << j), c).wait_recv()
            value = value + zrecv[j, t // (2 << j), c].astype(F32)
        return value

    loop(n // 4, lambda j: scatter(other(0, 2 * j), other(0, 2 * j + 1)))
    loop(n // 4, lambda j: scatter(kept(0, 2 * j), kept(0, 2 * j + 1)))

    def reduce_step(k, c):
        count = n >> (k + 1)

        def send(i):
            h = lax.rem(z // (2 << k) + i + count // 2, count)
            t = other(k, h)
            zsend[t, c] = total(t, k, c).astype(BF16)
            z_copy(k, h, c).start()

        loop(count, send)

    for c in range(parts):
        reduce_step(0, c)

    rows[...] = jnp.zeros_like(rows)

    def turn(k):
        psf_t[span(k, pixels), 0:bins] = psf_ref[k].T
        psf_t[span(k, pixels), bins:2 * bins] = psf_ref[k + fold].T

    loop(fold, turn, unroll=True)

    def mark_t(i):
        size = 128
        lane = lax.broadcasted_iota(jnp.int32, (size, slots), 1)
        slot = cols[span(i, size), 1:2]
        onehot_t[span(i, size), :] = jnp.where(lane == slot, 1.0, 0.0).astype(BF16)

    loop(entries // 128, mark_t, unroll=True)

    for k in range(1, steps):
        for c in range(parts):
            reduce_step(k, c)
    for load in loads:
        load.wait()

    def pass_on(t, k, c):
        for j in reversed(range(k)):
            g_copy(j, t // (2 << j), c).start()
        p_copy(t, c).start()

    for c in range(parts):
        at = pl.ds(c * sub, sub)
        out = bad[at, :].astype(F32) * (total(z, steps, c) - obs[at, :].astype(F32))
        resid[z, my_rows(c), :] = out.astype(BF16)
        pass_on(z, steps, c)

    def gathered(h, where):
        pair = jnp.concatenate([resid[2 * h, where, :], resid[2 * h + 1, where, :]], axis=1)

        def block(i):
            at = span(i, step_rows)
            got = dot(onehot_t[at, where], pair)
            tile = jnp.broadcast_to(cols[at, 0:1], (step_rows, pixels))
            value = jnp.where(tile == 2 * h, got[:, 0:pixels], 0.0)
            value = jnp.where(tile == 2 * h + 1, got[:, pixels:2 * pixels], value)
            rows[at, :] = rows[at, :] + value

        loop(entries // step_rows, block, unroll=True)

    for k in reversed(range(1, steps)):
        count = n >> (k + 1)
        for c in range(parts):
            def arrive(i):
                h = lax.rem(z // (2 << k) + i, count)
                g_copy(k, h, c).wait_recv()
                pass_on(other(k, h), k, c)

            loop(count, arrive)

    def last(i):
        h = lax.rem(z // 2 + i, n // 2)
        for c in range(parts):
            g_copy(0, h, c).wait_recv()
            p_copy(other(0, h), c).start()
            gathered(h, my_rows(c))
        for c in range(parts):
            p_copy(2 * h, c, arriving=True).wait_recv()
            p_copy(2 * h + 1, c, arriving=True).wait_recv()
            gathered(h, peer_rows(c))

    loop(n // 2, last)

    def backward(i):
        at = span(i, step_rows)
        col = cols[at, :]
        kind = jnp.broadcast_to(col[:, 4:5], (step_rows, pixels))
        term = through(rows[at, :], kind, psf_t)
        block = jnp.broadcast_to(col[:, 3:4], (step_rows, bins))
        terms[at, :] = spread(term, block, blocks)

    loop(entries // step_rows, backward, unroll=True)

    share = sources // nd

    wing = wide // 2

    def summed(to, w):
        row = lax.broadcasted_iota(jnp.int32, (share, entries), 0) + to * share
        member = jnp.where(row == src_ref[...], 1.0, 0.0).astype(BF16)
        return dot(member, terms[:, w * wing:(w + 1) * wing])

    def d_copy(k, w):
        to = lax.rem(d + k, nd)
        return copy(
            dsend.at[k - 1, w], drecv.at[k - 1, w], ds_sem.at[k - 1, w], dr_sem.at[k - 1, w],
            {"dither": to},
        )

    for k in range(1, nd):
        for w in range(2):
            dsend[k - 1, w] = summed(lax.rem(d + k, nd), w).astype(BF16)
            d_copy(k, w).start()
    for w in range(2):
        grad_ref[:, w * wing:(w + 1) * wing] = summed(d, w)
    res_ref[...] = resid[z]
    for w in range(2):
        value = grad_ref[:, w * wing:(w + 1) * wing]
        for k in range(1, nd):
            d_copy(k, w).wait_recv()
            value = value + drecv[k - 1, w].astype(F32)
        grad_ref[:, w * wing:(w + 1) * wing] = value

    for k in range(1, nd):
        for w in range(2):
            d_copy(k, w).wait_send()
    for c in range(parts):
        loop(n, lambda t: f_copy(t, c).wait_send())
        loop(n, lambda t: p_copy(t, c).wait_send())
        for k in range(steps):
            loop(n >> (k + 1), lambda h: z_copy(k, h, c).wait_send())
            loop(n >> (k + 1), lambda h: g_copy(k, h, c).wait_send())


def place(grad_from, res_from, grad_to, res_to, sems):
    moves = [
        pltpu.make_async_copy(grad_from, grad_to, sems.at[0]),
        pltpu.make_async_copy(res_from, res_to, sems.at[1]),
    ]
    for move in moves:
        move.start()
    for move in moves:
        move.wait()


def per_device(
    n, nd, spectra, psf_blocks, observed, bad_mask,
    trace_tile, trace_slot, trace_source, trace_block, psf_index,
):
    entries = trace_slot.shape[0]
    slots, pixels = observed.shape[1:]
    kinds, bins, _ = psf_blocks.shape
    sources, wide = spectra.shape
    half = slots // 2
    steps = n.bit_length() - 1
    parts = 2
    sub = half // parts
    row = lambda a: a.reshape(1, entries)
    dma = pltpu.SemaphoreType.DMA
    grad, res = pl.pallas_call(
        functools.partial(kernel, (n, nd, steps, parts)),
        out_shape=(
            jax.ShapeDtypeStruct((sources // nd, wide), F32),
            jax.ShapeDtypeStruct((slots, pixels), BF16),
        ),
        in_specs=(
            [pl.BlockSpec(memory_space=pltpu.VMEM)] * 2
            + [pl.BlockSpec(memory_space=pl.ANY)] * 2
            + [pl.BlockSpec(memory_space=pltpu.VMEM)] * 5
        ),
        out_specs=[pl.BlockSpec(memory_space=pltpu.VMEM)] * 2,
        scratch_shapes=[
            pltpu.VMEM((entries, 8), jnp.int32),
            pltpu.VMEM((entries, pixels), BF16),
            pltpu.VMEM((entries, 2 * pixels), BF16),
            pltpu.VMEM((slots, entries), BF16),
            pltpu.VMEM((entries, slots), BF16),
            pltpu.VMEM((kinds // 2 * bins, 2 * pixels), BF16),
            pltpu.VMEM((kinds // 2 * pixels, 2 * bins), BF16),
            pltpu.VMEM((n, parts, sub, pixels), F32),
            pltpu.VMEM((n, parts, sub, pixels), BF16),
            pltpu.VMEM((n, parts, sub, pixels), BF16),
            pltpu.VMEM((steps, n // 2, parts, sub, pixels), BF16),
            pltpu.VMEM((n, parts, sub, pixels), BF16),
            pltpu.VMEM((n, slots, pixels), BF16),
            pltpu.VMEM((entries, pixels), F32),
            pltpu.VMEM((entries, wide), BF16),
            pltpu.VMEM((nd - 1, 2, sources // nd, wide // 2), BF16),
            pltpu.VMEM((nd - 1, 2, sources // nd, wide // 2), BF16),
            pltpu.VMEM((half, pixels), BF16),
            pltpu.VMEM((half, pixels), jnp.int32),
            dma((n, parts)), dma((n, parts)),
            dma((n, parts)), dma((steps, n // 2, parts)),
            dma((steps, n // 2, parts)), dma((steps, n // 2, parts)),
            dma((n, parts)), dma((n, parts)),
            dma((nd - 1, 2)), dma((nd - 1, 2)), dma((2,)),
        ],
        compiler_params=pltpu.CompilerParams(
            collective_id=0, has_side_effects=True, vmem_limit_bytes=56 * 1024 * 1024
        ),
        cost_estimate=pl.CostEstimate(
            flops=2 * entries * pixels * (2 * kinds * bins + 2 * n * slots + 8 * sources),
            bytes_accessed=2 * 1024 * 1024,
            transcendentals=0,
        ),
    )(
        spectra, psf_blocks, observed[0], bad_mask[0],
        row(trace_tile), row(trace_slot), row(trace_source), row(trace_block), row(psf_index),
    )
    grad, res = pl.pallas_call(
        place,
        out_shape=(
            jax.ShapeDtypeStruct(grad.shape, F32), jax.ShapeDtypeStruct(res.shape, BF16)
        ),
        in_specs=[pl.BlockSpec(memory_space=pl.ANY)] * 2,
        out_specs=[pl.BlockSpec(memory_space=pl.ANY)] * 2,
        scratch_shapes=[dma((2,))],
        compiler_params=pltpu.CompilerParams(vmem_limit_bytes=60 * 1024 * 1024),
    )(grad, res)
    return grad, res[None]


def solution(mesh):
    in_specs = (
        P(("groups", "tile"), "band"),
        P(),
        P(("groups", "dither"), "tile", None),
        P(("groups", "dither"), "tile", None),
        P(("groups", "tile", "dither", "band"), None),
        P(("groups", "tile", "dither", "band")),
        P(("groups", "tile", "dither", "band"), None),
        P(("groups", "tile", "dither", "band")),
        P(("groups", "tile", "dither", "band")),
    )
    out_specs = (P(("groups", "tile", "dither"), "band"), P(("groups", "dither"), "tile", None))
    fn = functools.partial(per_device, mesh.shape["tile"], mesh.shape["dither"])
    return jax.shard_map(fn, mesh=mesh, in_specs=in_specs, out_specs=out_specs, check_vma=False)
```

time: 42.4 us -> 56 us (1.32)
  Pallas kernels: 39.1 us -> 55.2 us
  local copies, waits for them, and re-layouts: 2.42 us -> 0 us
    pallas_call x1 -> x2, Pallas kernels: 39.1 us -> 55.2 us  [the longest x1 38.2 us: per_device(): pl.pallas_call(functools.partial(kernel, (n, nd, steps, parts)), out_shap...]
    unnamed x4 -> x0, local copies, waits for them, and re-layouts: 2.42 us -> none
where the time goes in v5:
time: 56 us; the launch traced here: 55.8 us
  Pallas kernels  55.2 us (99%)
  between operations  0.64 us (1%)
    pallas_call x1, Pallas kernels, per_device(): pl.pallas_call(functools.partial(kernel, (n, nd, steps, parts)), out_shap...  38.2 us
    pallas_call x1, Pallas kernels, per_device(): pl.pallas_call(place, out_shape=(jax.ShapeDtypeStruct(grad.shape, F32), j...  17 us

profile of v5, /device:TPU:0, one launch (start us, length us, event | category | flops | bytes accessed | tf_op | source)
XLA Modules:
  0.0 55.8 jit_solution(18416003986752564176)
XLA Ops:
  0.6 38.2 %shard_map.104 = (f32[128,512]{1,0:T(8,128)}, bf16[1024,128]{1,0:T(8,128)(2,1)}) custom-call(bf16[256,512]{1,0:T(8,128)(2,1)} %spectra_ref.1, bf16[16,128,128]{2,1,0:T(8,128)(2,1)} %psf_ref.1, bf16[1024,128]{1,0:T(8,128)(2,1)} %bitcast.9, s32[1024,128]{1,0:T(8,128)} %bitcast.8, s32[1,1024]{1,0:T(1,128)} %bitcast.11, s32[1,1024]{1,0:T(1,128)} %bitcast.12, ...), custom_call_target="tpu_custom_call" | custom-call | flops 3758096384 | bytes 2097152 | tf_op jit(solution)/shard_map/pallas_call | solution.py:347
  38.8 17.0 %shard_map.105 = (f32[128,512]{1,0:T(8,128)}, bf16[1024,128]{1,0:T(8,128)(2,1)}) custom-call(f32[128,512]{1,0:T(8,128)} %get-tuple-element.6.grad_from, bf16[1024,128]{1,0:T(8,128)(2,1)} %get-tuple-element.7.res_from), custom_call_target="tpu_custom_call" | custom-call | tf_op jit(solution)/shard_map/pallas_call | solution.py:397

commit v6 on v5

--- a/solution.py
+++ b/solution.py
@@ -156,23 +156,15 @@
         masked[:, 0:pixels] = jnp.where(tile == t, trace, 0.0).astype(BF16)
         masked[:, pixels:2 * pixels] = jnp.where(tile == u, trace, 0.0).astype(BF16)
 
+        part = dot(onehot[theirs, :], masked[...]).astype(BF16)
+        fsend[t] = part[:, 0:pixels].reshape(parts, sub, pixels)
+        fsend[u] = part[:, pixels:2 * pixels].reshape(parts, sub, pixels)
         for c in range(parts):
-            def away(i):
-                at = span(i, step_rows, (1 - b) * half + c * sub)
-                part = dot(onehot[at, :], masked[...]).astype(BF16)
-                fsend[t, c, span(i, step_rows), :] = part[:, 0:pixels]
-                fsend[u, c, span(i, step_rows), :] = part[:, pixels:2 * pixels]
-
-            loop(sub // step_rows, away, unroll=True)
             f_copy(t, c).start()
             f_copy(u, c).start()
-        for c in range(parts):
-            def here(i):
-                part = dot(onehot[span(i, step_rows, b * half + c * sub), :], masked[...])
-                own[t, c, span(i, step_rows), :] = part[:, 0:pixels]
-                own[u, c, span(i, step_rows), :] = part[:, pixels:2 * pixels]
-
-            loop(sub // step_rows, here, unroll=True)
+        part = dot(onehot[mine, :], masked[...])
+        own[t] = part[:, 0:pixels].reshape(parts, sub, pixels)
+        own[u] = part[:, pixels:2 * pixels].reshape(parts, sub, pixels)
 
     def total(t, k, c):
         f_copy(t, c).wait_recv()
@@ -236,14 +228,14 @@
         pair = jnp.concatenate([resid[2 * h, where, :], resid[2 * h + 1, where, :]], axis=1)
 
         def block(i):
-            at = span(i, step_rows)
+            at = span(i, entries // 2)
             got = dot(onehot_t[at, where], pair)
-            tile = jnp.broadcast_to(cols[at, 0:1], (step_rows, pixels))
+            tile = jnp.broadcast_to(cols[at, 0:1], (entries // 2, pixels))
             value = jnp.where(tile == 2 * h, got[:, 0:pixels], 0.0)
             value = jnp.where(tile == 2 * h + 1, got[:, pixels:2 * pixels], value)
             rows[at, :] = rows[at, :] + value
 
-        loop(entries // step_rows, block, unroll=True)
+        loop(2, block, unroll=True)
 
     for k in reversed(range(1, steps)):
         count = n >> (k + 1)
@@ -319,15 +311,9 @@
             loop(n >> (k + 1), lambda h: g_copy(k, h, c).wait_send())
 
 
-def place(grad_from, res_from, grad_to, res_to, sems):
-    moves = [
-        pltpu.make_async_copy(grad_from, grad_to, sems.at[0]),
-        pltpu.make_async_copy(res_from, res_to, sems.at[1]),
-    ]
-    for move in moves:
-        move.start()
-    for move in moves:
-        move.wait()
+def place(grad_from, res_from, grad_to, res_to):
+    grad_to[...] = grad_from[...]
+    res_to[...] = res_from[...]
 
 
 def per_device(
@@ -352,7 +338,7 @@
         ),
         in_specs=(
             [pl.BlockSpec(memory_space=pltpu.VMEM)] * 2
-            + [pl.BlockSpec(memory_space=pl.ANY)] * 2
+            + [pl.BlockSpec(memory_space=pltpu.HBM)] * 2
             + [pl.BlockSpec(memory_space=pltpu.VMEM)] * 5
         ),
         out_specs=[pl.BlockSpec(memory_space=pltpu.VMEM)] * 2,
@@ -399,10 +385,8 @@
         out_shape=(
             jax.ShapeDtypeStruct(grad.shape, F32), jax.ShapeDtypeStruct(res.shape, BF16)
         ),
-        in_specs=[pl.BlockSpec(memory_space=pl.ANY)] * 2,
-        out_specs=[pl.BlockSpec(memory_space=pl.ANY)] * 2,
-        scratch_shapes=[dma((2,))],
-        compiler_params=pltpu.CompilerParams(vmem_limit_bytes=60 * 1024 * 1024),
+        in_specs=[pl.BlockSpec(memory_space=pltpu.VMEM)] * 2,
+        out_specs=[pl.BlockSpec(memory_space=pltpu.VMEM)] * 2,
     )(grad, res)
     return grad, res[None]
 

time: 56 us -> 40.2 us (0.72)
  Pallas kernels: 55.2 us -> 39.4 us
    pallas_call x1, Pallas kernels: 17 us -> 1.84 us  [per_device(): pl.pallas_call(place, out_shape=(jax.ShapeDtypeStruct(grad.shape, F32), j...]
    pallas_call x1, Pallas kernels: 38.2 us -> 37.6 us  [per_device(): pl.pallas_call(functools.partial(kernel, (n, nd, steps, parts)), out_shap...]
where the time goes in v6:
time: 40.2 us; the launch traced here: 40 us
  Pallas kernels  39.4 us (98%)
  between operations  0.64 us (2%)
    pallas_call x1, Pallas kernels, per_device(): pl.pallas_call(functools.partial(kernel, (n, nd, steps, parts)), out_shap...  37.6 us
    pallas_call x1, Pallas kernels, per_device(): pl.pallas_call(place, out_shape=(jax.ShapeDtypeStruct(grad.shape, F32), j...  1.84 us

profile of v6, /device:TPU:0, one launch (start us, length us, event | category | flops | bytes accessed | tf_op | source)
XLA Modules:
  0.0 40.0 jit_solution(4965213670569176654)
XLA Ops:
  0.6 37.6 %shard_map.104 = (f32[128,512]{1,0:T(8,128)}, bf16[1024,128]{1,0:T(8,128)(2,1)}) custom-call(bf16[256,512]{1,0:T(8,128)(2,1)} %spectra_ref.1, bf16[16,128,128]{2,1,0:T(8,128)(2,1)} %psf_ref.1, bf16[1024,128]{1,0:T(8,128)(2,1)} %bitcast.9, s32[1024,128]{1,0:T(8,128)} %bitcast.8, s32[1,1024]{1,0:T(1,128)} %bitcast.11, s32[1,1024]{1,0:T(1,128)} %bitcast.12, ...), custom_call_target="tpu_custom_call" | custom-call | flops 3758096384 | bytes 2097152 | tf_op jit(solution)/shard_map/pallas_call | solution.py:333
  38.2 1.8 %shard_map.105 = (f32[128,512]{1,0:T(8,128)}, bf16[1024,128]{1,0:T(8,128)(2,1)}) custom-call(f32[128,512]{1,0:T(8,128)} %get-tuple-element.6.grad_from, bf16[1024,128]{1,0:T(8,128)(2,1)} %get-tuple-element.7.res_from), custom_call_target="tpu_custom_call" | custom-call | tf_op jit(solution)/shard_map/pallas_call | solution.py:383

commit v7 on v6

--- a/solution.py
+++ b/solution.py
@@ -32,7 +32,7 @@
     sources, wide = spectra_ref.shape
     blocks = wide // bins
     fold = kinds // 2
-    step_rows = min(256, entries, sub)
+    step_rows = min(256, entries)
     z = lax.axis_index("tile")
     b = lax.axis_index("band")
     d = lax.axis_index("dither")
@@ -207,22 +207,36 @@
 
     loop(entries // 128, mark_t, unroll=True)
 
-    for k in range(1, steps):
-        for c in range(parts):
-            reduce_step(k, c)
-    for load in loads:
-        load.wait()
-
     def pass_on(t, k, c):
         for j in reversed(range(k)):
             g_copy(j, t // (2 << j), c).start()
         p_copy(t, c).start()
 
-    for c in range(parts):
+    def finish(c):
+        if c == 0:
+            for load in loads:
+                load.wait()
         at = pl.ds(c * sub, sub)
         out = bad[at, :].astype(F32) * (total(z, steps, c) - obs[at, :].astype(F32))
         resid[z, my_rows(c), :] = out.astype(BF16)
         pass_on(z, steps, c)
+
+    def arrive_step(k, c):
+        count = n >> (k + 1)
+
+        def arrive(i):
+            h = lax.rem(z // (2 << k) + i, count)
+            g_copy(k, h, c).wait_recv()
+            pass_on(other(k, h), k, c)
+
+        loop(count, arrive)
+
+    stages = [functools.partial(reduce_step, k) for k in range(1, steps)]
+    stages += [finish] + [functools.partial(arrive_step, k) for k in reversed(range(1, steps))]
+    for i in range(parts + len(stages) - 1):
+        for j, stage in enumerate(stages):
+            if 0 <= i - j < parts:
+                stage(i - j)
 
     def gathered(h, where):
         pair = jnp.concatenate([resid[2 * h, where, :], resid[2 * h + 1, where, :]], axis=1)
@@ -237,26 +251,18 @@
 
         loop(2, block, unroll=True)
 
-    for k in reversed(range(1, steps)):
-        count = n >> (k + 1)
-        for c in range(parts):
-            def arrive(i):
-                h = lax.rem(z // (2 << k) + i, count)
-                g_copy(k, h, c).wait_recv()
-                pass_on(other(k, h), k, c)
-
-            loop(count, arrive)
-
     def last(i):
         h = lax.rem(z // 2 + i, n // 2)
         for c in range(parts):
             g_copy(0, h, c).wait_recv()
             p_copy(other(0, h), c).start()
-            gathered(h, my_rows(c))
+            if c % 2:
+                gathered(h, span(c // 2, 2 * sub, b * half))
         for c in range(parts):
             p_copy(2 * h, c, arriving=True).wait_recv()
             p_copy(2 * h + 1, c, arriving=True).wait_recv()
-            gathered(h, peer_rows(c))
+            if c % 2:
+                gathered(h, span(c // 2, 2 * sub, (1 - b) * half))
 
     loop(n // 2, last)
 
@@ -326,7 +332,7 @@
     sources, wide = spectra.shape
     half = slots // 2
     steps = n.bit_length() - 1
-    parts = 2
+    parts = 4
     sub = half // parts
     row = lambda a: a.reshape(1, entries)
     dma = pltpu.SemaphoreType.DMA

time: 40.2 us -> 43.8 us (1.090)
  Pallas kernels: 39.4 us -> 43 us
    pallas_call x1, Pallas kernels: 37.6 us -> 41.1 us  [per_device(): pl.pallas_call(functools.partial(kernel, (n, nd, steps, parts)), out_shap...]
where the time goes in v7:
time: 43.8 us; the launch traced here: 43.6 us
  Pallas kernels  43 us (98%)
  between operations  0.64 us (1%)
    pallas_call x1, Pallas kernels, per_device(): pl.pallas_call(functools.partial(kernel, (n, nd, steps, parts)), out_shap...  41.1 us
    pallas_call x1, Pallas kernels, per_device(): pl.pallas_call(place, out_shape=(jax.ShapeDtypeStruct(grad.shape, F32), j...  1.84 us

profile of v7, /device:TPU:0, one launch (start us, length us, event | category | flops | bytes accessed | tf_op | source)
XLA Modules:
  0.0 43.6 jit_solution(11378764764919594706)
XLA Ops:
  0.6 41.1 %shard_map.104 = (f32[128,512]{1,0:T(8,128)}, bf16[1024,128]{1,0:T(8,128)(2,1)}) custom-call(bf16[256,512]{1,0:T(8,128)(2,1)} %spectra_ref.1, bf16[16,128,128]{2,1,0:T(8,128)(2,1)} %psf_ref.1, bf16[1024,128]{1,0:T(8,128)(2,1)} %bitcast.9, s32[1024,128]{1,0:T(8,128)} %bitcast.8, s32[1,1024]{1,0:T(1,128)} %bitcast.11, s32[1,1024]{1,0:T(1,128)} %bitcast.12, ...), custom_call_target="tpu_custom_call" | custom-call | flops 3758096384 | bytes 2097152 | tf_op jit(solution)/shard_map/pallas_call | solution.py:339
  41.8 1.8 %shard_map.105 = (f32[128,512]{1,0:T(8,128)}, bf16[1024,128]{1,0:T(8,128)(2,1)}) custom-call(f32[128,512]{1,0:T(8,128)} %get-tuple-element.6.grad_from, bf16[1024,128]{1,0:T(8,128)(2,1)} %get-tuple-element.7.res_from), custom_call_target="tpu_custom_call" | custom-call | tf_op jit(solution)/shard_map/pallas_call | solution.py:389

commit v8 on v7

--- a/solution.py
+++ b/solution.py
@@ -124,17 +124,14 @@
     def my_rows(c):
         return span(c, sub, b * half)
 
-    def peer_rows(c):
-        return span(c, sub, (1 - b) * half)
-
     def copy(src, dst, send, recv, where):
         return pltpu.make_async_remote_copy(
             src_ref=src, dst_ref=dst, send_sem=send, recv_sem=recv,
             device_id=where, device_id_type=MESH,
         )
 
-    def f_copy(t, c):
-        return copy(fsend.at[t, c], frecv.at[t, c], fs_sem.at[t, c], fr_sem.at[t, c], peer)
+    def f_copy(t):
+        return copy(fsend.at[t], frecv.at[t], fs_sem.at[t], fr_sem.at[t], peer)
 
     def z_copy(k, h, c):
         t = other(k, h)
@@ -146,9 +143,9 @@
         block = resid.at[kept(k, h), my_rows(c)]
         return copy(block, block, gs_sem.at[k, h, c], gr_sem.at[k, h, c], partner(k))
 
-    def p_copy(t, c, arriving=False):
-        block = resid.at[t, peer_rows(c) if arriving else my_rows(c)]
-        return copy(block, block, ps_sem.at[t, c], pr_sem.at[t, c], peer)
+    def p_copy(t, arriving=False):
+        block = resid.at[t, theirs if arriving else mine]
+        return copy(block, block, ps_sem.at[t], pr_sem.at[t], peer)
 
     def scatter(t, u):
         tile = jnp.broadcast_to(cols[:, 0:1], (entries, pixels))
@@ -159,15 +156,15 @@
         part = dot(onehot[theirs, :], masked[...]).astype(BF16)
         fsend[t] = part[:, 0:pixels].reshape(parts, sub, pixels)
         fsend[u] = part[:, pixels:2 * pixels].reshape(parts, sub, pixels)
-        for c in range(parts):
-            f_copy(t, c).start()
-            f_copy(u, c).start()
+        f_copy(t).start()
+        f_copy(u).start()
         part = dot(onehot[mine, :], masked[...])
         own[t] = part[:, 0:pixels].reshape(parts, sub, pixels)
         own[u] = part[:, pixels:2 * pixels].reshape(parts, sub, pixels)
 
     def total(t, k, c):
-        f_copy(t, c).wait_recv()
+        if c == 0:
+            f_copy(t).wait_recv()
         value = own[t, c] + frecv[t, c].astype(F32)
         for j in range(k):
             z_copy(j, t // (2 << j), c).wait_recv()
@@ -210,7 +207,8 @@
     def pass_on(t, k, c):
         for j in reversed(range(k)):
             g_copy(j, t // (2 << j), c).start()
-        p_copy(t, c).start()
+        if c == parts - 1:
+            p_copy(t).start()
 
     def finish(c):
         if c == 0:
@@ -255,14 +253,11 @@
         h = lax.rem(z // 2 + i, n // 2)
         for c in range(parts):
             g_copy(0, h, c).wait_recv()
-            p_copy(other(0, h), c).start()
-            if c % 2:
-                gathered(h, span(c // 2, 2 * sub, b * half))
-        for c in range(parts):
-            p_copy(2 * h, c, arriving=True).wait_recv()
-            p_copy(2 * h + 1, c, arriving=True).wait_recv()
-            if c % 2:
-                gathered(h, span(c // 2, 2 * sub, (1 - b) * half))
+        p_copy(other(0, h)).start()
+        gathered(h, mine)
+        p_copy(2 * h, arriving=True).wait_recv()
+        p_copy(2 * h + 1, arriving=True).wait_recv()
+        gathered(h, theirs)
 
     loop(n // 2, last)
 
@@ -309,9 +304,9 @@
     for k in range(1, nd):
         for w in range(2):
             d_copy(k, w).wait_send()
+    loop(n, lambda t: f_copy(t).wait_send())
+    loop(n, lambda t: p_copy(t).wait_send())
     for c in range(parts):
-        loop(n, lambda t: f_copy(t, c).wait_send())
-        loop(n, lambda t: p_copy(t, c).wait_send())
         for k in range(steps):
             loop(n >> (k + 1), lambda h: z_copy(k, h, c).wait_send())
             loop(n >> (k + 1), lambda h: g_copy(k, h, c).wait_send())
@@ -332,7 +327,7 @@
     sources, wide = spectra.shape
     half = slots // 2
     steps = n.bit_length() - 1
-    parts = 4
+    parts = 2
     sub = half // parts
     row = lambda a: a.reshape(1, entries)
     dma = pltpu.SemaphoreType.DMA
@@ -368,10 +363,10 @@
             pltpu.VMEM((nd - 1, 2, sources // nd, wide // 2), BF16),
             pltpu.VMEM((half, pixels), BF16),
             pltpu.VMEM((half, pixels), jnp.int32),
-            dma((n, parts)), dma((n, parts)),
+            dma((n,)), dma((n,)),
             dma((n, parts)), dma((steps, n // 2, parts)),
             dma((steps, n // 2, parts)), dma((steps, n // 2, parts)),
-            dma((n, parts)), dma((n, parts)),
+            dma((n,)), dma((n,)),
             dma((nd - 1, 2)), dma((nd - 1, 2)), dma((2,)),
         ],
         compiler_params=pltpu.CompilerParams(

time: 43.8 us -> 40.6 us (0.927)
  Pallas kernels: 43 us -> 39.8 us
    pallas_call x1, Pallas kernels: 41.1 us -> 38 us  [per_device(): pl.pallas_call(functools.partial(kernel, (n, nd, steps, parts)), out_shap...]
where the time goes in v8:
time: 40.6 us; the launch traced here: 40.4 us
  Pallas kernels  39.8 us (98%)
  between operations  0.64 us (2%)
    pallas_call x1, Pallas kernels, per_device(): pl.pallas_call(functools.partial(kernel, (n, nd, steps, parts)), out_shap...  38 us
    pallas_call x1, Pallas kernels, per_device(): pl.pallas_call(place, out_shape=(jax.ShapeDtypeStruct(grad.shape, F32), j...  1.84 us

profile of v8, /device:TPU:0, one launch (start us, length us, event | category | flops | bytes accessed | tf_op | source)
XLA Modules:
  0.0 40.4 jit_solution(8154651278217708505)
XLA Ops:
  0.6 38.0 %shard_map.104 = (f32[128,512]{1,0:T(8,128)}, bf16[1024,128]{1,0:T(8,128)(2,1)}) custom-call(bf16[256,512]{1,0:T(8,128)(2,1)} %spectra_ref.1, bf16[16,128,128]{2,1,0:T(8,128)(2,1)} %psf_ref.1, bf16[1024,128]{1,0:T(8,128)(2,1)} %bitcast.9, s32[1024,128]{1,0:T(8,128)} %bitcast.8, s32[1,1024]{1,0:T(1,128)} %bitcast.11, s32[1,1024]{1,0:T(1,128)} %bitcast.12, ...), custom_call_target="tpu_custom_call" | custom-call | flops 3758096384 | bytes 2097152 | tf_op jit(solution)/shard_map/pallas_call | solution.py:334
  38.6 1.8 %shard_map.105 = (f32[128,512]{1,0:T(8,128)}, bf16[1024,128]{1,0:T(8,128)(2,1)}) custom-call(f32[128,512]{1,0:T(8,128)} %get-tuple-element.6.grad_from, bf16[1024,128]{1,0:T(8,128)(2,1)} %get-tuple-element.7.res_from), custom_call_target="tpu_custom_call" | custom-call | tf_op jit(solution)/shard_map/pallas_call | solution.py:384
